TPU v7x, 32 devices: a whole 2x2x4 slice. The times are simulated.
32 devices in a mesh: sx: 4 (over y, x), sy: 2 (over core), sz: 4 (over z).
Axes of the slice: x: 2, y: 2, z: 4, core: 2. Of those that a mesh axis runs over, the one named last changes fastest.
Arguments:
- density: bfloat16 [4, 32, 16, 64], P(None, 'sx', 'sy', 'sz'), may hold values from -6 to 6
- conv1_weight: bfloat16 [32, 3, 3, 3, 4], replicated, may hold values from -0.625 to 0.625
- conv1_bias: float32 [32], replicated, may hold values from -3 to 3
- conv1_probe: bfloat16 [32, 3, 3, 3, 4], replicated, may hold values from -0.625 to 0.625
- conv2_weight: bfloat16 [32, 3, 3, 3, 32], replicated, may hold values from -0.21875 to 0.21875
- conv2_bias: float32 [32], replicated, may hold values from -3 to 3
- conv2_probe: bfloat16 [32, 3, 3, 3, 32], replicated, may hold values from -0.21875 to 0.21875
- lift_weight: bfloat16 [256, 4, 4, 4, 32], replicated, may hold values from -0.125 to 0.125
- lift_bias: float32 [256], replicated, may hold values from -3 to 3
- lift_probe: bfloat16 [256, 4, 4, 4, 32], replicated, may hold values from -0.125 to 0.125
- conv3_weight: bfloat16 [256, 3, 3, 3, 256], P(None, None, None, None, ('sx', 'sy')), may hold values from -0.109375 to 0.109375
- conv3_bias: float32 [256], P(('sx', 'sy')), may hold values from -3 to 3
- conv3_probe: bfloat16 [256, 3, 3, 3, 256], P(None, None, None, None, ('sx', 'sy')), may hold values from -0.109375 to 0.109375
Outputs:
- features: bfloat16 [256, 8, 4, 16], P(('sx', 'sy'), None, None, 'sz')
- tangent: bfloat16 [256, 8, 4, 16], P(('sx', 'sy'), None, None, 'sz')
All inputs are finite; a program needn't handle non-finite values.
Results may differ from a plain program's by a relative error of at most 0.013.
Values may be sent and summed in bfloat16 or wider, within the bound.
A program may use at most 64 MiB of HBM per device.

v0:
```python
import jax
import jax.numpy as jnp
from jax import lax
from jax.sharding import PartitionSpec as P


def with_halo(cells, sides, width):
    for axis, dim in sides:
        count = lax.axis_size(axis)
        ends = count - 1
        head = lax.slice_in_dim(cells, 0, width, axis=dim)
        tail = lax.slice_in_dim(cells, cells.shape[dim] - width, cells.shape[dim], axis=dim)
        cells = jnp.concatenate(
            [
                lax.ppermute(tail, axis, [(i, (i + 1) % count) for i in range(ends)]),
                cells,
                lax.ppermute(head, axis, [((i + 1) % count, i) for i in range(ends)]),
            ],
            axis=dim,
        )
    return cells


def swish_pair(preact, direction):
    sigmoid_value = jax.nn.sigmoid(preact)
    derivative = sigmoid_value * (1.0 + preact * (1.0 - sigmoid_value))
    return (preact * sigmoid_value, derivative * direction)


def cells(volume, weight, stride, out_order):
    return lax.conv_general_dilated(
        volume,
        weight,
        (stride, stride, stride),
        "VALID",
        dimension_numbers=("NCDHW", "ODHWI", out_order),
        preferred_element_type=jnp.float32,
    )


def per_channel(vector):
    return vector[:, None, None, None]


def inside_range(length, offset, whole):
    position = jnp.arange(length, dtype=jnp.int32) - 1 + offset
    return ((position >= 0) & (position < whole)).astype(jnp.float32)


def body(
    density,
    conv1_weight,
    conv1_bias,
    conv1_probe,
    conv2_weight,
    conv2_bias,
    conv2_probe,
    lift_weight,
    lift_bias,
    lift_probe,
    conv3_weight,
    conv3_bias,
    conv3_probe,
):
    channels_in, span_x, span_y, span_z = density.shape
    width_one = conv1_weight.shape[0]
    width_three = lift_weight.shape[0]
    both_first = jnp.concatenate([conv1_weight, conv1_probe], 0)
    padded = with_halo(density, (("sx", 1), ("sy", 2), ("sz", 3)), 2)
    pre_both = cells(padded[None], both_first, 1, "NCDHW")[0]
    hidden, probe = swish_pair(pre_both[:width_one] + per_channel(conv1_bias), pre_both[width_one:])
    inside_x = inside_range(span_x + 2, lax.axis_index("sx") * span_x, span_x * lax.axis_size("sx"))
    inside_y = inside_range(span_y + 2, lax.axis_index("sy") * span_y, span_y * lax.axis_size("sy"))
    inside_z = inside_range(span_z + 2, lax.axis_index("sz") * span_z, span_z * lax.axis_size("sz"))
    inside = inside_x[:, None, None] * inside_y[None, :, None] * inside_z[None, None, :]
    pair = jnp.stack(
        [(hidden * inside).astype(jnp.bfloat16), (probe * inside).astype(jnp.bfloat16)]
    )
    both = cells(pair, conv2_weight, 1, "NCDHW")
    extra = cells(pair[:1], conv2_probe, 1, "NCDHW")[0]
    hidden, probe = swish_pair(both[0] + per_channel(conv2_bias), both[1] + extra)
    pair = jnp.stack([hidden.astype(jnp.bfloat16), probe.astype(jnp.bfloat16)])
    both = cells(pair, lift_weight, 4, "NCDHW")
    extra = cells(pair[:1], lift_probe, 4, "NCDHW")[0]
    hidden, probe = swish_pair(both[0] + per_channel(lift_bias), both[1] + extra)
    stacked = jnp.stack([hidden.astype(jnp.bfloat16), probe.astype(jnp.bfloat16)])
    coarse_x, coarse_y, coarse_z = (stacked.shape[2], stacked.shape[3], stacked.shape[4])
    across = lax.axis_size("sx")
    downward = lax.axis_size("sy")
    per_device = width_three // (across * downward)
    rimmed = with_halo(stacked, (("sx", 2), ("sy", 3), ("sz", 4)), 1)
    zero_sums = jnp.zeros((width_three, coarse_x, coarse_y, coarse_z), jnp.float32)
    pieces = (
        lax.all_gather(conv3_weight, ("sx", "sy"), axis=4, tiled=True),
        lax.all_gather(conv3_probe, ("sx", "sy"), axis=4, tiled=True),
    )
    piece_count = pieces[0].shape[4]
    channel_block = lax.slice_in_dim(rimmed, 0, piece_count, axis=1)
    pair_sums = cells(channel_block, pieces[0], 1, "NCDHW")
    probe_sums = cells(channel_block[:1], pieces[1], 1, "NCDHW")[0]
    primal_sum = zero_sums + pair_sums[0]
    change_sum = zero_sums + pair_sums[1] + probe_sums
    totals = jnp.stack([primal_sum, change_sum]).reshape(
        2, across, downward, per_device, coarse_x, coarse_y, coarse_z
    )
    received = lax.all_to_all(
        lax.all_to_all(totals.astype(jnp.bfloat16), "sx", split_axis=1, concat_axis=4, tiled=True),
        "sy",
        split_axis=2,
        concat_axis=5,
        tiled=True,
    ).astype(totals.dtype)
    primal = received[0, 0, 0]
    change = received[1, 0, 0]
    features = (primal + per_channel(conv3_bias)).astype(jnp.bfloat16)
    return (features, change.astype(jnp.bfloat16))


def solution(mesh):
    placed = (
        P(None, "sx", "sy", "sz"),
        P(),
        P(),
        P(),
        P(),
        P(),
        P(),
        P(),
        P(),
        P(),
        P(None, None, None, None, ("sx", "sy")),
        P(("sx", "sy")),
        P(None, None, None, None, ("sx", "sy")),
    )
    return jax.shard_map(
        body,
        mesh=mesh,
        in_specs=placed,
        out_specs=(P(("sx", "sy"), None, None, "sz"), P(("sx", "sy"), None, None, "sz")),
        check_vma=False,
    )
```

profile of v0, /device:TPU:0, one launch (start us, length us, event | category | flops | bytes accessed | tf_op | source)
XLA Modules:
  0.0 115.4 jit_solution(15831784697483188397)
XLA Ops:
  7.2 0.7 all-gather.3.cloned.1.call-update
  8.0 0.7 fusion.59
  8.7 4.8 %collective-permute-start = (bf16[4,2,8,16]{3,2,1,0:T(8,128)(2,1)S(1)}, bf16[4,2,8,16]{3,2,1,0:T(8,128)(2,1)S(1)}, u32[]{:S(2)}, u32[]{:S(2)}) collective-permute-start(bf16[4,2,8,16]{3,2,1,0:T(8,128)(2,1)S(1)} %get-tuple-element.26), channel_id=1, source_target_pairs={{0,8},{8,16},{16,24},{1,9},{9,17},{17,25},{2,10},{10,18},{18,26},{... | collective-permute-start | bytes 6152 | tf_op jit(solution)/shard_map/ppermute | solution.py:15
  13.5 1.3 %collective-permute-start.1 = (bf16[4,2,8,16]{3,2,1,0:T(8,128)(2,1)S(1)}, bf16[4,2,8,16]{3,2,1,0:T(8,128)(2,1)S(1)}, u32[]{:S(2)}, u32[]{:S(2)}) collective-permute-start(bf16[4,2,8,16]{3,2,1,0:T(8,128)(2,1)S(1)} %get-tuple-element.25), channel_id=1, source_target_pairs={{8,0},{16,8},{24,16},{9,1},{17,9},{25,17},{10,2},{18,10},{26,18},{... | collective-permute-start | bytes 6152 | tf_op jit(solution)/shard_map/ppermute | solution.py:17
  15.0 0.9 constant_dynamic-update-slice_fusion.1
  15.8 3.4 %collective-permute-done.1 = bf16[4,2,8,16]{3,2,1,0:T(8,128)(2,1)S(1)} collective-permute-done((bf16[4,2,8,16]{3,2,1,0:T(8,128)(2,1)S(1)}, bf16[4,2,8,16]{3,2,1,0:T(8,128)(2,1)S(1)}, u32[]{:S(2)}, u32[]{:S(2)}) %collective-permute-start.1) | collective-permute-done | bytes 2080 | tf_op jit(solution)/shard_map/ppermute | solution.py:17
  19.2 1.3 %collective-permute-start.2 = (bf16[4,12,2,16]{3,2,1,0:T(2,128)(2,1)S(1)}, bf16[4,12,2,16]{3,2,1,0:T(2,128)(2,1)S(1)}, u32[]{:S(2)}, u32[]{:S(2)}) collective-permute-start(bf16[4,12,2,16]{3,2,1,0:T(2,128)(2,1)S(1)} %get-tuple-element.18), channel_id=1, source_target_pairs={{0,4},{1,5},{2,6},{3,7},{8,12},{9,13},{10,14},{11,15},{16,20},{17,... | collective-permute-start | bytes 9224 | tf_op jit(solution)/shard_map/ppermute | solution.py:15
  20.5 1.3 %collective-permute-start.3 = (bf16[4,12,2,16]{3,2,1,0:T(2,128)(2,1)S(1)}, bf16[4,12,2,16]{3,2,1,0:T(2,128)(2,1)S(1)}, u32[]{:S(2)}, u32[]{:S(2)}) collective-permute-start(bf16[4,12,2,16]{3,2,1,0:T(2,128)(2,1)S(1)} %get-tuple-element.19), channel_id=1, source_target_pairs={{4,0},{5,1},{6,2},{7,3},{12,8},{13,9},{14,10},{15,11},{20,16},{21,... | collective-permute-start | bytes 9224 | tf_op jit(solution)/shard_map/ppermute | solution.py:17
  21.8 1.8 %collective-permute-done.3 = bf16[4,12,2,16]{3,2,1,0:T(2,128)(2,1)S(1)} collective-permute-done((bf16[4,12,2,16]{3,2,1,0:T(2,128)(2,1)S(1)}, bf16[4,12,2,16]{3,2,1,0:T(2,128)(2,1)S(1)}, u32[]{:S(2)}, u32[]{:S(2)}) %collective-permute-start.3) | collective-permute-done | bytes 3104 | tf_op jit(solution)/shard_map/ppermute | solution.py:17
  23.6 0.1 pad_maximum_fusion.1
  23.7 0.1 fusion.55
  23.9 3.5 %collective-permute-start.4 = (bf16[4,12,12,2]{3,2,1,0:T(8,128)(2,1)S(1)}, bf16[4,12,12,2]{3,2,1,0:T(8,128)(2,1)S(1)}, u32[]{:S(2)}, u32[]{:S(2)}) collective-permute-start(bf16[4,12,12,2]{3,2,1,0:T(8,128)(2,1)S(1)} %get-tuple-element.16), channel_id=1, source_target_pairs={{0,1},{1,2},{2,3},{4,5},{5,6},{6,7},{8,9},{9,10},{10,11},{12,13},{... | collective-permute-start | bytes 6920 | tf_op jit(solution)/shard_map/ppermute | solution.py:15
  27.4 1.3 %collective-permute-start.5 = (bf16[4,12,12,2]{3,2,1,0:T(8,128)(2,1)S(1)}, bf16[4,12,12,2]{3,2,1,0:T(8,128)(2,1)S(1)}, u32[]{:S(2)}, u32[]{:S(2)}) collective-permute-start(bf16[4,12,12,2]{3,2,1,0:T(8,128)(2,1)S(1)} %get-tuple-element.17), channel_id=1, source_target_pairs={{1,0},{2,1},{3,2},{5,4},{6,5},{7,6},{9,8},{10,9},{11,10},{13,12},{... | collective-permute-start | bytes 6920 | tf_op jit(solution)/shard_map/ppermute | solution.py:17
  28.8 3.0 %collective-permute-done.4 = bf16[4,12,12,2]{3,2,1,0:T(8,128)(2,1)S(1)} collective-permute-done((bf16[4,12,12,2]{3,2,1,0:T(8,128)(2,1)S(1)}, bf16[4,12,12,2]{3,2,1,0:T(8,128)(2,1)S(1)}, u32[]{:S(2)}, u32[]{:S(2)}) %collective-permute-start.4) | collective-permute-done | bytes 2336 | tf_op jit(solution)/shard_map/ppermute | solution.py:15
  31.8 4.1 %collective-permute-done.5 = bf16[4,12,12,2]{3,2,1,0:T(8,128)(2,1)S(1)} collective-permute-done((bf16[4,12,12,2]{3,2,1,0:T(8,128)(2,1)S(1)}, bf16[4,12,12,2]{3,2,1,0:T(8,128)(2,1)S(1)}, u32[]{:S(2)}, u32[]{:S(2)}) %collective-permute-start.5) | collective-permute-done | bytes 2336 | tf_op jit(solution)/shard_map/ppermute | solution.py:17
  35.9 0.3 maximum_bitcast_fusion.1
  36.3 0.4 copy.78
  36.7 0.1 pad.clone
  36.8 1.0 copy.51
  37.8 0.2 slice.112
  38.1 2.7 %convolution_select_fusion = f32[10,10,8,3,64]{4,2,3,1,0:T(8,128)S(1)} fusion(bf16[4,12,12,1,7,2]{4,0,5,2,1,3:T(4,128)(2,1)S(1)} %slice.112, bf16[4,12,12,1,8,3]{4,0,5,2,1,3:T(4,128)(2,1)S(1)} %copy.51, pred[8,3]{0,1:T(4,128)(4,1)S(1)} %copy-done.13, bf16[32,3,3,3,4]{0,4,3,2,1:T(4,128)(2,1)S(1)} %copy-done.9, bf16[32,3,3,3,4]{0,4,3,2,1:T(4,128)(2,1)S(1)} %copy-done.10), kind=kOutput, calls=%fused_computation.10 | convolution fusion | flops 33497088 | bytes 672024 | tf_op jit(solution)/shard_map/conv_general_dilated | solution.py:31
  40.8 1.6 %fusion.11 = (f32[10,10,8,3,32]{4,2,3,1,0:T(8,128)S(1)}, f32[10,10,8,3,32]{4,2,3,1,0:T(8,128)}) fusion(f32[10,10,8,3,64]{4,2,3,1,0:T(8,128)S(1)} %convolution_select_fusion, f32[32]{0:T(128)S(1)} %copy-done.3), kind=kLoop, calls=%fused_computation.20 | loop fusion | flops 768000 | bytes 1228928 | tf_op jit(solution)/shard_map/mul | solution.py:27
  42.4 0.5 copy.52
  42.9 1.5 %reshape.102 = f32[10,10,1,24,32]{4,3,1,0,2:T(8,128)} reshape(f32[10,10,8,3,32]{4,3,2,1,0:T(4,128)S(1)} %copy.52) | data formatting | bytes 614400 | tf_op jit(solution)/shard_map/mul | solution.py:27
  44.4 1.8 %copy.53 = f32[10,10,8,3,32]{4,3,2,1,0:T(4,128)S(1)} copy(f32[10,10,8,3,32]{4,2,3,1,0:T(8,128)} %get-tuple-element.13) | data formatting | bytes 614400 | tf_op jit(solution)/shard_map/mul | solution.py:27
  46.2 1.4 %reshape.104 = f32[10,10,1,24,32]{4,3,1,0,2:T(8,128)} reshape(f32[10,10,8,3,32]{4,3,2,1,0:T(4,128)S(1)} %copy.53) | data formatting | bytes 614400 | tf_op jit(solution)/shard_map/mul | solution.py:27
  47.6 2.9 %fusion.33 = (bf16[32,10,10,1,18]{0,4,2,1,3:T(8,128)(2,1)S(1)}, bf16[1,32,10,10,18]{1,4,3,2,0:T(8,128)(2,1)S(1)}, bf16[1,32,10,10,18]{1,4,3,2,0:T(8,128)(2,1)}) fusion(f32[10,10,18]{2,1,0:T(8,128)S(1)} %broadcast_multiply_fusion, f32[10,10,1,24,32]{4,3,1,0,2:T(8,128)} %reshape.102, f32[10,10,1,24,32]{4,3,1,0,2:T(8,128)} %reshape.104), kind=kLoop, calls=%fused_computation.50 | loop fusion | flops 230400 | bytes 813600 | tf_op jit(solution)/shard_map/convert_element_type | solution.py:77
  50.5 0.1 pad.4
  50.7 0.4 reshape.114
  51.3 0.7 copy-done.7
  52.0 1.4 %convolution_select_fusion.1 = f32[8,8,8,3,32]{4,2,3,1,0:T(8,128)S(1)} fusion(bf16[32,3,3,3,32]{4,0,3,2,1:T(8,128)(2,1)S(1)} %copy-done.7, bf16[32,10,10,1,7,2]{0,4,5,2,1,3:T(8,128)(2,1)S(1)} %slice.121, bf16[32,10,10,1,8,3]{0,4,5,2,1,3:T(8,128)(2,1)S(1)} %copy.59, pred[8,3]{0,1:T(4,128)(4,1)S(1)} %copy-done.12), kind=kOutput, calls=%fused_computation.11 | convolution fusion | flops 85751808 | bytes 495128 | tf_op jit(solution)/shard_map/conv_general_dilated | solution.py:31
  53.4 0.1 copy.60
  53.6 0.9 copy-done.1
  54.5 0.3 maximum_bitcast_fusion
  54.8 0.7 copy.79
  55.5 1.1 pad.2.clone
  56.6 0.5 slice.117
  57.2 2.4 %fusion = bf16[32,10,10,2,8,5]{0,3,5,4,2,1:T(2,128)(2,1)S(1)} fusion(bf16[32,10,10,2,7,2]{0,3,5,4,2,1:T(2,128)(2,1)S(1)} %slice.117, bf16[32,10,10,2,8,3]{0,3,5,4,2,1:T(2,128)(2,1)S(1)} %bitcast.70), kind=kLoop, calls=%fused_computation.1 | loop fusion | flops 1536000 | bytes 998400 | tf_op jit(solution)/shard_map/conv_general_dilated | solution.py:31
  59.6 2.3 %fusion.6 = f32[8,8,16,3,32]{4,2,3,1,0:T(8,128)S(1)} fusion(bf16[32,3,3,3,32]{4,0,3,2,1:T(8,128)(2,1)S(1)} %copy-done.8, bf16[32,10,10,2,8,5]{0,3,5,4,2,1:T(2,128)(2,1)S(1)} %fusion, pred[16,3]{0,1:T(4,128)(4,1)S(1)} %copy-done.11), kind=kOutput, calls=%fused_computation.9 | convolution fusion | flops 169967616 | bytes 960560 | tf_op jit(solution)/shard_map/conv_general_dilated | solution.py:31
  61.9 0.5 copy.56
  62.5 0.2 copy.122
  62.7 0.5 copy-done.4
  63.1 0.3 multiply_convert_fusion
  63.4 0.1 pad_maximum_fusion
  63.6 1.1 fusion.27
  64.8 0.8 fusion.29
  65.7 4.4 %collective-permute-start.6 = (bf16[2,256,1,2,4]{1,4,3,2,0:T(4,128)(2,1)S(1)}, bf16[2,256,1,2,4]{1,4,3,2,0:T(4,128)(2,1)S(1)}, u32[]{:S(2)}, u32[]{:S(2)}) collective-permute-start(bf16[2,256,1,2,4]{1,4,3,2,0:T(4,128)(2,1)S(1)} %get-tuple-element.33), channel_id=1, source_target_pairs={{0,8},{8,16},{16,24},{1,9},{9,17},{17,25},{2,10},{10,18},{18,26},{... | collective-permute-start | bytes 24584 | tf_op jit(solution)/shard_map/ppermute | solution.py:15
  70.1 1.3 %collective-permute-start.7 = (bf16[2,256,1,2,4]{1,4,3,2,0:T(4,128)(2,1)S(1)}, bf16[2,256,1,2,4]{1,4,3,2,0:T(4,128)(2,1)S(1)}, u32[]{:S(2)}, u32[]{:S(2)}) collective-permute-start(bf16[2,256,1,2,4]{1,4,3,2,0:T(4,128)(2,1)S(1)} %get-tuple-element.34), channel_id=1, source_target_pairs={{8,0},{16,8},{24,16},{9,1},{17,9},{25,17},{10,2},{18,10},{26,18},{... | collective-permute-start | bytes 24584 | tf_op jit(solution)/shard_map/ppermute | solution.py:17
  71.4 4.3 %collective-permute-done.7 = bf16[2,256,1,2,4]{1,4,3,2,0:T(4,128)(2,1)S(1)} collective-permute-done((bf16[2,256,1,2,4]{1,4,3,2,0:T(4,128)(2,1)S(1)}, bf16[2,256,1,2,4]{1,4,3,2,0:T(4,128)(2,1)S(1)}, u32[]{:S(2)}, u32[]{:S(2)}) %collective-permute-start.7) | collective-permute-done | bytes 8224 | tf_op jit(solution)/shard_map/ppermute | solution.py:17
  75.8 1.3 %collective-permute-start.8 = (bf16[2,256,4,1,4]{1,4,3,2,0:T(4,128)(2,1)S(1)}, bf16[2,256,4,1,4]{1,4,3,2,0:T(4,128)(2,1)S(1)}, u32[]{:S(2)}, u32[]{:S(2)}) collective-permute-start(bf16[2,256,4,1,4]{1,4,3,2,0:T(4,128)(2,1)S(1)} %get-tuple-element.27), channel_id=1, source_target_pairs={{0,4},{1,5},{2,6},{3,7},{8,12},{9,13},{10,14},{11,15},{16,20},{17,... | collective-permute-start | bytes 49160 | tf_op jit(solution)/shard_map/ppermute | solution.py:15
  77.1 1.3 %collective-permute-start.9 = (bf16[2,256,4,1,4]{1,4,3,2,0:T(4,128)(2,1)S(1)}, bf16[2,256,4,1,4]{1,4,3,2,0:T(4,128)(2,1)S(1)}, u32[]{:S(2)}, u32[]{:S(2)}) collective-permute-start(bf16[2,256,4,1,4]{1,4,3,2,0:T(4,128)(2,1)S(1)} %get-tuple-element.28), channel_id=1, source_target_pairs={{4,0},{5,1},{6,2},{7,3},{12,8},{13,9},{14,10},{15,11},{20,16},{21,... | collective-permute-start | bytes 49160 | tf_op jit(solution)/shard_map/ppermute | solution.py:17
  78.4 1.8 %collective-permute-done.9 = bf16[2,256,4,1,4]{1,4,3,2,0:T(4,128)(2,1)S(1)} collective-permute-done((bf16[2,256,4,1,4]{1,4,3,2,0:T(4,128)(2,1)S(1)}, bf16[2,256,4,1,4]{1,4,3,2,0:T(4,128)(2,1)S(1)}, u32[]{:S(2)}, u32[]{:S(2)}) %collective-permute-start.9) | collective-permute-done | bytes 16416 | tf_op jit(solution)/shard_map/ppermute | solution.py:17
  80.3 3.4 %collective-permute-start.10 = (bf16[2,256,4,4,1]{1,4,3,2,0:T(2,128)(2,1)S(1)}, bf16[2,256,4,4,1]{1,4,3,2,0:T(2,128)(2,1)S(1)}, u32[]{:S(2)}, u32[]{:S(2)}) collective-permute-start(bf16[2,256,4,4,1]{1,4,3,2,0:T(2,128)(2,1)S(1)} %get-tuple-element.23), channel_id=1, source_target_pairs={{0,1},{1,2},{2,3},{4,5},{5,6},{6,7},{8,9},{9,10},{10,11},{12,13},{... | collective-permute-start | bytes 49160 | tf_op jit(solution)/shard_map/ppermute | solution.py:15
  83.8 1.3 %collective-permute-start.11 = (bf16[2,256,4,4,1]{1,4,3,2,0:T(2,128)(2,1)S(1)}, bf16[2,256,4,4,1]{1,4,3,2,0:T(2,128)(2,1)S(1)}, u32[]{:S(2)}, u32[]{:S(2)}) collective-permute-start(bf16[2,256,4,4,1]{1,4,3,2,0:T(2,128)(2,1)S(1)} %get-tuple-element.24), channel_id=1, source_target_pairs={{1,0},{2,1},{3,2},{5,4},{6,5},{7,6},{9,8},{10,9},{11,10},{13,12},{... | collective-permute-start | bytes 49160 | tf_op jit(solution)/shard_map/ppermute | solution.py:17
  85.1 0.3 collective-permute-done.10
  85.3 4.2 %collective-permute-done.11 = bf16[2,256,4,4,1]{1,4,3,2,0:T(2,128)(2,1)S(1)} collective-permute-done((bf16[2,256,4,4,1]{1,4,3,2,0:T(2,128)(2,1)S(1)}, bf16[2,256,4,4,1]{1,4,3,2,0:T(2,128)(2,1)S(1)}, u32[]{:S(2)}, u32[]{:S(2)}) %collective-permute-start.11) | collective-permute-done | bytes 16416 | tf_op jit(solution)/shard_map/ppermute | solution.py:17
  89.7 2.8 %fusion.37 = f32[2,256,2,2,4]{1,0,4,3,2:T(2,128)S(1)} fusion(bf16[256,3,3,3,256]{0,4,3,2,1:T(8,128)(2,1)} %all-gather.3.cloned.1.call-done, bf16[2,256,4,4,6]{1,4,3,2,0:T(8,128)(2,1)S(1)} %pad_maximum_fusion.2), kind=kOutput, calls=%fused_computation.54 | convolution fusion | flops 113246208 | bytes 3670016 | tf_op jit(solution)/shard_map/conv_general_dilated | solution.py:31
  92.6 2.9 %fusion.44 = (bf16[256,2,2,4]{0,3,2,1:T(4,128)(2,1)S(1)}, bf16[256,2,2,4]{0,3,2,1:T(4,128)(2,1)S(1)}) fusion(f32[2,256,2,2,4]{1,0,4,3,2:T(2,128)S(1)} %fusion.37, bf16[256,3,3,3,256]{0,4,3,2,1:T(8,128)(2,1)} %all-gather.5.cloned.1.call-done, bf16[1,256,4,4,6]{1,4,3,2,0:T(8,128)(2,1)S(1)} %slice.133), kind=kOutput, calls=%fused_computation.69 | convolution fusion | flops 56635392 | bytes 3637248 | tf_op jit(solution)/shard_map/conv_general_dilated | solution.py:31
  95.7 0.1 reshape.135
  95.9 7.2 %all_to_all.27 = bf16[4,2,1024]{2,1,0:T(2,128)(2,1)S(1)} all-to-all(bf16[4,2,1024]{2,1,0:T(2,128)(2,1)S(1)} %reshape.135), channel_id=1, replica_groups=mesh['sx'=4,'sy'=2,'sz'=4] {'sx'}, dimensions={0} | all-to-all | bytes 32768 | tf_op jit(solution)/shard_map/all_to_all | solution.py:107
  103.3 0.1 reshape.137
  103.4 3.7 %all_to_all.28 = bf16[2,2,2048]{2,1,0:T(2,128)(2,1)S(1)} all-to-all(bf16[2,2,2048]{2,1,0:T(2,128)(2,1)S(1)} %reshape.137), channel_id=1, replica_groups=mesh['sx'=4,'sy'=2,'sz'=4] {'sy'}, dimensions={0} | all-to-all | bytes 32768 | tf_op jit(solution)/shard_map/all_to_all | solution.py:106
  107.3 0.6 copy.73
  107.9 0.6 fusion.39
  (65 shorter events, 1.8 us)
Async XLA Ops:
  7.2 56.4 %copy-start = (bf16[256,4,4,4,32]{0,4,3,2,1:T(8,128)(2,1)S(1)}, bf16[256,4,4,4,32]{0,4,3,2,1:T(8,128)(2,1)}, u32[]{:S(2)}) copy-start(bf16[256,4,4,4,32]{0,4,3,2,1:T(8,128)(2,1)} %param.20) | copy-start | bytes 3145732
  7.2 82.5 %all-gather.3.cloned.1.call-start = ((), (), s32[]{:S(2)}) async-start(), calls=%async_computation.2 | async-start | bytes 3981312 | tf_op jit(solution)/shard_map/all_gather | solution.py:94
  7.9 84.7 %all-gather.5.cloned.1.call-start = ((), (), s32[]{:S(2)}) async-start(), calls=%async_computation.3 | async-start | bytes 3981312 | tf_op jit(solution)/shard_map/all_gather | solution.py:95
  8.7 6.3 %collective-permute-start = (bf16[4,2,8,16]{3,2,1,0:T(8,128)(2,1)S(1)}, bf16[4,2,8,16]{3,2,1,0:T(8,128)(2,1)S(1)}, u32[]{:S(2)}, u32[]{:S(2)}) collective-permute-start(bf16[4,2,8,16]{3,2,1,0:T(8,128)(2,1)S(1)} %get-tuple-element.26), channel_id=1, source_target_pairs={{0,8},{8,16},{16,24},{1,9},{9,17},{17,25},{2,10},{10,18},{18,26},{... | collective-permute-start | bytes 6152 | tf_op jit(solution)/shard_map/ppermute | solution.py:15
  13.5 5.6 %collective-permute-start.1 = (bf16[4,2,8,16]{3,2,1,0:T(8,128)(2,1)S(1)}, bf16[4,2,8,16]{3,2,1,0:T(8,128)(2,1)S(1)}, u32[]{:S(2)}, u32[]{:S(2)}) collective-permute-start(bf16[4,2,8,16]{3,2,1,0:T(8,128)(2,1)S(1)} %get-tuple-element.25), channel_id=1, source_target_pairs={{8,0},{16,8},{24,16},{9,1},{17,9},{25,17},{10,2},{18,10},{26,18},{... | collective-permute-start | bytes 6152 | tf_op jit(solution)/shard_map/ppermute | solution.py:17
  19.2 2.6 %collective-permute-start.2 = (bf16[4,12,2,16]{3,2,1,0:T(2,128)(2,1)S(1)}, bf16[4,12,2,16]{3,2,1,0:T(2,128)(2,1)S(1)}, u32[]{:S(2)}, u32[]{:S(2)}) collective-permute-start(bf16[4,12,2,16]{3,2,1,0:T(2,128)(2,1)S(1)} %get-tuple-element.18), channel_id=1, source_target_pairs={{0,4},{1,5},{2,6},{3,7},{8,12},{9,13},{10,14},{11,15},{16,20},{17,... | collective-permute-start | bytes 9224 | tf_op jit(solution)/shard_map/ppermute | solution.py:15
  20.5 3.1 %collective-permute-start.3 = (bf16[4,12,2,16]{3,2,1,0:T(2,128)(2,1)S(1)}, bf16[4,12,2,16]{3,2,1,0:T(2,128)(2,1)S(1)}, u32[]{:S(2)}, u32[]{:S(2)}) collective-permute-start(bf16[4,12,2,16]{3,2,1,0:T(2,128)(2,1)S(1)} %get-tuple-element.19), channel_id=1, source_target_pairs={{4,0},{5,1},{6,2},{7,3},{12,8},{13,9},{14,10},{15,11},{20,16},{21,... | collective-permute-start | bytes 9224 | tf_op jit(solution)/shard_map/ppermute | solution.py:17
  23.9 8.0 %collective-permute-start.4 = (bf16[4,12,12,2]{3,2,1,0:T(8,128)(2,1)S(1)}, bf16[4,12,12,2]{3,2,1,0:T(8,128)(2,1)S(1)}, u32[]{:S(2)}, u32[]{:S(2)}) collective-permute-start(bf16[4,12,12,2]{3,2,1,0:T(8,128)(2,1)S(1)} %get-tuple-element.16), channel_id=1, source_target_pairs={{0,1},{1,2},{2,3},{4,5},{5,6},{6,7},{8,9},{9,10},{10,11},{12,13},{... | collective-permute-start | bytes 6920 | tf_op jit(solution)/shard_map/ppermute | solution.py:15
  27.4 8.6 %collective-permute-start.5 = (bf16[4,12,12,2]{3,2,1,0:T(8,128)(2,1)S(1)}, bf16[4,12,12,2]{3,2,1,0:T(8,128)(2,1)S(1)}, u32[]{:S(2)}, u32[]{:S(2)}) collective-permute-start(bf16[4,12,12,2]{3,2,1,0:T(8,128)(2,1)S(1)} %get-tuple-element.17), channel_id=1, source_target_pairs={{1,0},{2,1},{3,2},{5,4},{6,5},{7,6},{9,8},{10,9},{11,10},{13,12},{... | collective-permute-start | bytes 6920 | tf_op jit(solution)/shard_map/ppermute | solution.py:17
  28.8 9.3 %copy-start.9 = (bf16[32,3,3,3,4]{0,4,3,2,1:T(4,128)(2,1)S(1)}, bf16[32,3,3,3,4]{0,4,3,2,1:T(4,128)(2,1)}, u32[]{:S(2)}) copy-start(bf16[32,3,3,3,4]{0,4,3,2,1:T(4,128)(2,1)} %param.16) | copy-start | bytes 20740
  28.8 9.3 %copy-start.10 = (bf16[32,3,3,3,4]{0,4,3,2,1:T(4,128)(2,1)S(1)}, bf16[32,3,3,3,4]{0,4,3,2,1:T(4,128)(2,1)}, u32[]{:S(2)}) copy-start(bf16[32,3,3,3,4]{0,4,3,2,1:T(4,128)(2,1)} %param.14) | copy-start | bytes 20740
  28.8 9.3 %copy-start.13 = (pred[8,3]{0,1:T(4,128)(4,1)S(1)}, pred[8,3]{0,1:T(4,128)(4,1)}, u32[]{:S(2)}) copy-start(pred[8,3]{0,1:T(4,128)(4,1)} %constant.46) | copy-start | bytes 76
  38.1 2.7 %copy-start.3 = (f32[32]{0:T(128)S(1)}, f32[32]{0:T(128)}, u32[]{:S(2)}) copy-start(f32[32]{0:T(128)} %param.15) | copy-start | bytes 388
  51.1 0.9 copy-start.7
  51.1 0.9 copy-start.12
  53.4 1.1 copy-start.1
  57.1 2.4 %copy-start.8 = (bf16[32,3,3,3,32]{4,0,3,2,1:T(8,128)(2,1)S(1)}, bf16[32,3,3,3,32]{4,0,3,2,1:T(8,128)(2,1)}, u32[]{:S(2)}) copy-start(bf16[32,3,3,3,32]{4,0,3,2,1:T(8,128)(2,1)} %param.17) | copy-start | bytes 165892
  57.1 2.4 %copy-start.11 = (pred[16,3]{0,1:T(4,128)(4,1)S(1)}, pred[16,3]{0,1:T(4,128)(4,1)}, u32[]{:S(2)}) copy-start(pred[16,3]{0,1:T(4,128)(4,1)} %constant.45) | copy-start | bytes 148
  62.5 0.7 copy-start.4
  63.4 1.3 %copy-start.6 = (bf16[256,4,4,4,32]{0,4,3,2,1:T(8,128)(2,1)S(1)}, bf16[256,4,4,4,32]{0,4,3,2,1:T(8,128)(2,1)}, u32[]{:S(2)}) copy-start(bf16[256,4,4,4,32]{0,4,3,2,1:T(8,128)(2,1)} %param.22) | copy-start | bytes 3145732
  64.7 0.9 copy-start.2
  65.7 5.7 %collective-permute-start.6 = (bf16[2,256,1,2,4]{1,4,3,2,0:T(4,128)(2,1)S(1)}, bf16[2,256,1,2,4]{1,4,3,2,0:T(4,128)(2,1)S(1)}, u32[]{:S(2)}, u32[]{:S(2)}) collective-permute-start(bf16[2,256,1,2,4]{1,4,3,2,0:T(4,128)(2,1)S(1)} %get-tuple-element.33), channel_id=1, source_target_pairs={{0,8},{8,16},{16,24},{1,9},{9,17},{17,25},{2,10},{10,18},{18,26},{... | collective-permute-start | bytes 24584 | tf_op jit(solution)/shard_map/ppermute | solution.py:15
  70.1 5.7 %collective-permute-start.7 = (bf16[2,256,1,2,4]{1,4,3,2,0:T(4,128)(2,1)S(1)}, bf16[2,256,1,2,4]{1,4,3,2,0:T(4,128)(2,1)S(1)}, u32[]{:S(2)}, u32[]{:S(2)}) collective-permute-start(bf16[2,256,1,2,4]{1,4,3,2,0:T(4,128)(2,1)S(1)} %get-tuple-element.34), channel_id=1, source_target_pairs={{8,0},{16,8},{24,16},{9,1},{17,9},{25,17},{10,2},{18,10},{26,18},{... | collective-permute-start | bytes 24584 | tf_op jit(solution)/shard_map/ppermute | solution.py:17
  75.8 2.6 %collective-permute-start.8 = (bf16[2,256,4,1,4]{1,4,3,2,0:T(4,128)(2,1)S(1)}, bf16[2,256,4,1,4]{1,4,3,2,0:T(4,128)(2,1)S(1)}, u32[]{:S(2)}, u32[]{:S(2)}) collective-permute-start(bf16[2,256,4,1,4]{1,4,3,2,0:T(4,128)(2,1)S(1)} %get-tuple-element.27), channel_id=1, source_target_pairs={{0,4},{1,5},{2,6},{3,7},{8,12},{9,13},{10,14},{11,15},{16,20},{17,... | collective-permute-start | bytes 49160 | tf_op jit(solution)/shard_map/ppermute | solution.py:15
  77.1 3.1 %collective-permute-start.9 = (bf16[2,256,4,1,4]{1,4,3,2,0:T(4,128)(2,1)S(1)}, bf16[2,256,4,1,4]{1,4,3,2,0:T(4,128)(2,1)S(1)}, u32[]{:S(2)}, u32[]{:S(2)}) collective-permute-start(bf16[2,256,4,1,4]{1,4,3,2,0:T(4,128)(2,1)S(1)} %get-tuple-element.28), channel_id=1, source_target_pairs={{4,0},{5,1},{6,2},{7,3},{12,8},{13,9},{14,10},{15,11},{20,16},{21,... | collective-permute-start | bytes 49160 | tf_op jit(solution)/shard_map/ppermute | solution.py:17
  80.3 5.0 %collective-permute-start.10 = (bf16[2,256,4,4,1]{1,4,3,2,0:T(2,128)(2,1)S(1)}, bf16[2,256,4,4,1]{1,4,3,2,0:T(2,128)(2,1)S(1)}, u32[]{:S(2)}, u32[]{:S(2)}) collective-permute-start(bf16[2,256,4,4,1]{1,4,3,2,0:T(2,128)(2,1)S(1)} %get-tuple-element.23), channel_id=1, source_target_pairs={{0,1},{1,2},{2,3},{4,5},{5,6},{6,7},{8,9},{9,10},{10,11},{12,13},{... | collective-permute-start | bytes 49160 | tf_op jit(solution)/shard_map/ppermute | solution.py:15
  83.8 5.8 %collective-permute-start.11 = (bf16[2,256,4,4,1]{1,4,3,2,0:T(2,128)(2,1)S(1)}, bf16[2,256,4,4,1]{1,4,3,2,0:T(2,128)(2,1)S(1)}, u32[]{:S(2)}, u32[]{:S(2)}) collective-permute-start(bf16[2,256,4,4,1]{1,4,3,2,0:T(2,128)(2,1)S(1)} %get-tuple-element.24), channel_id=1, source_target_pairs={{1,0},{2,1},{3,2},{5,4},{6,5},{7,6},{9,8},{10,9},{11,10},{13,12},{... | collective-permute-start | bytes 49160 | tf_op jit(solution)/shard_map/ppermute | solution.py:17
  92.5 15.4 %copy-start.5 = (f32[32]{0:T(128)S(1)}, f32[32]{0:T(128)}, u32[]{:S(2)}) copy-start(f32[32]{0:T(128)} %param.24) | copy-start | bytes 388
Sparse Core Ops, SparseCore 0:
  9.9 36.6 all-gather.2
  48.5 34.0 all-gather.4
where the time goes:
time: 116 us; the launch traced here: 115 us
  starting transfers between devices  26.5 us (23%)
  waiting for transfers between devices  23.7 us (20%)
  local copies, waits for them, and re-layouts  16.3 us (14%)
  between operations  14.7 us (13%)
  matrix products  14 us (12%)
  blocking collectives  10.9 us (9%)
  other arithmetic  9.22 us (8%)
    ppermute x6, waiting for transfers between devices, with_halo(): lax.ppermute(head, axis, [((i + 1) % count, i) for i in range(ends)])  19.6 us
    ppermute x6, starting transfers between devices, with_halo(): lax.ppermute(tail, axis, [(i, (i + 1) % count) for i in range(ends)])  18.7 us
    conv_general_dilated x7, matrix products, cells(): lax.conv_general_dilated(volume, weight, (stride, stride, stride), 'VALID...  14 us
    ppermute x6, starting transfers between devices, with_halo(): lax.ppermute(head, axis, [((i + 1) % count, i) for i in range(ends)])  7.75 us
    all_to_all x1, blocking collectives, body(): lax.all_to_all(totals.astype(jnp.bfloat16), 'sx', split_axis=1, concat_ax...  7.22 us
    unnamed x38, local copies, waits for them, and re-layouts  5.36 us
    mul x4, local copies, waits for them, and re-layouts, swish_pair(): return (preact * sigmoid_value, derivative * direction)  5.14 us
    all_to_all x1, blocking collectives, body(): lax.all_to_all(lax.all_to_all(totals.astype(jnp.bfloat16), 'sx', split_ax...  3.72 us
  transfers between devices with their start and end apart: 14, of which 8 were waited for; matrix products, arithmetic and copies ran while one was open for 28% of the time, Pallas kernels for 0%

commit v1 on v0

v1 whole, which is shorter than its diff:
```python
import functools
import itertools

import jax
import jax.numpy as jnp
from jax import lax
from jax.experimental import pallas as pl
from jax.experimental.pallas import tpu as pltpu
from jax.sharding import PartitionSpec as P

MESH = pl.DeviceIdType.MESH
VMEM = pl.BlockSpec(memory_space=pltpu.VMEM)


def swish_pair(preact, direction):
    sigmoid_value = jax.nn.sigmoid(preact)
    derivative = sigmoid_value * (1.0 + preact * (1.0 - sigmoid_value))
    return (preact * sigmoid_value, derivative * direction)


def cells(volume, weight, stride, out_order):
    return lax.conv_general_dilated(
        volume,
        weight,
        (stride, stride, stride),
        "VALID",
        dimension_numbers=("NCDHW", "ODHWI", out_order),
        preferred_element_type=jnp.float32,
    )


def per_channel(vector):
    return vector[:, None, None, None]


def inside_range(length, offset, whole):
    position = jnp.arange(length, dtype=jnp.int32) - 1 + offset
    return ((position >= 0) & (position < whole)).astype(jnp.float32)


def positions(axes):
    return [lax.axis_index(a) for a in axes], [lax.axis_size(a) for a in axes]


OFFSETS = list(itertools.product((-1, 0, 1), repeat=3))


def one_hot(rows, columns, source, dim):
    shape = (rows, 1) if dim == 0 else (1, columns)
    want, ok = source(lax.broadcasted_iota(jnp.int32, shape, dim))
    want = jnp.where(ok, want, -1)
    return (lax.broadcasted_iota(jnp.int32, (rows, columns), 1 - dim) == want).astype(jnp.bfloat16)


def tiles_kernel(shape, width, tile, out, slots, send_sem, recv_sem):
    channels, span_x, span_y, span_z = shape
    wide_x, wide_y, wide_z = (span + 2 * width for span in (span_x, span_y, span_z))
    axes = ("sx", "sy", "sz")
    at, counts = positions(axes)

    def there(offset):
        ok = None
        for here, step, count in zip(at, offset, counts):
            if step:
                one = (here + step >= 0) & (here + step < count)
                ok = one if ok is None else ok & one
        return ok, tuple(here + step for here, step in zip(at, offset))

    others = [(i, o) for i, o in enumerate(OFFSETS) if any(o)]
    barrier = pltpu.get_barrier_semaphore()
    for _, offset in others:
        ok, target = there(offset)

        @pl.when(ok)
        def _():
            pl.semaphore_signal(barrier, inc=1, device_id=target, device_id_type=MESH)

    peers = 1
    for here, count in zip(at, counts):
        peers *= 1 + (here > 0).astype(jnp.int32) + (here < count - 1).astype(jnp.int32)
    pl.semaphore_wait(barrier, peers - 1)

    def copy(i, offset, target):
        return pltpu.make_async_remote_copy(
            src_ref=tile,
            dst_ref=slots.at[len(OFFSETS) - 1 - i],
            send_sem=send_sem.at[i],
            recv_sem=recv_sem.at[len(OFFSETS) - 1 - i],
            device_id=target,
            device_id_type=MESH,
        )

    for i, offset in others:
        ok, target = there(offset)

        @pl.when(ok)
        def _():
            copy(i, offset, target).start()

    slots[len(OFFSETS) // 2] = tile[...]
    cells_in = span_y * span_z

    def column(at_row):
        block, cell = at_row // cells_in, at_row % cells_in
        y = cell // span_z + width + (block // 3 - 1) * span_y
        z = cell % span_z + width + (block % 3 - 1) * span_z
        return y * wide_z + z, (y >= 0) & (y < wide_y) & (z >= 0) & (z < wide_z)

    def line(at_column):
        block, cell = at_column // (channels * span_x), at_column % (channels * span_x)
        x = cell % span_x + width + (block - 1) * span_x
        return cell // span_x * wide_x + x, (x >= 0) & (x < wide_x)

    columns = one_hot(9 * cells_in, wide_y * wide_z, column, 0)
    lines = one_hot(channels * wide_x, 3 * channels * span_x, line, 1)
    for i, offset in others:
        ok, target = there(offset)

        @pl.when(ok)
        def _():
            mirror = len(OFFSETS) - 1 - i
            copy(mirror, offset, target).wait_recv()

        @pl.when(jnp.logical_not(ok))
        def _():
            slots[i] = jnp.zeros_like(tile)

    dot = functools.partial(jnp.dot, preferred_element_type=jnp.float32)
    near = jnp.concatenate(
        [jnp.concatenate([slots[9 * i + j] for j in range(9)], axis=1) for i in range(3)], axis=0
    )
    near = dot(near, columns).astype(jnp.bfloat16)
    out[...] = dot(lines, near).astype(jnp.bfloat16)
    for i, offset in others:
        ok, target = there(offset)

        @pl.when(ok)
        def _():
            copy(i, offset, target).wait_send()


def with_halo(tile, width):
    channels, span_x, span_y, span_z = tile.shape
    wide_x, wide_y, wide_z = (span + 2 * width for span in (span_x, span_y, span_z))
    flat = (channels * span_x, span_y * span_z)
    return pl.pallas_call(
        functools.partial(tiles_kernel, tile.shape, width),
        out_shape=jax.ShapeDtypeStruct((channels * wide_x, wide_y * wide_z), tile.dtype),
        in_specs=[VMEM],
        out_specs=VMEM,
        scratch_shapes=[
            pltpu.VMEM((len(OFFSETS),) + flat, tile.dtype),
            pltpu.SemaphoreType.DMA((len(OFFSETS),)),
            pltpu.SemaphoreType.DMA((len(OFFSETS),)),
        ],
        compiler_params=pltpu.CompilerParams(collective_id=0, has_side_effects=True),
    )(tile.reshape(flat)).reshape(channels, wide_x, wide_y, wide_z)


def last_kernel(
    tile_shape, blocks, weight, probe, bias, out, lifted, sent, rows, copies, parts, landed,
    lift_send, lift_recv, part_send, part_recv,
):
    tx, ty, tz = tile_shape
    (ix, iy, iz), (nx, ny, nz) = positions(("sx", "sy", "sz"))
    groups = nx * ny
    me = ix * ny + iy
    width = weight.shape[0] // 27
    whole_y, depth = ny * ty, tz + 2
    step_y, step_x = depth, depth * (whole_y + 1)
    count = sent.shape[1]
    owned = out.shape[1]

    def place(k, dz):
        group = lax.rem(me + k, groups)
        return group, (lax.div(group, ny), lax.rem(group, ny), iz + dz)

    plan = [(dz, k) for dz in (0, -1, 1) for k in range(groups) if k or dz]

    def guarded(dz, action):
        if dz == 0:
            action()
        else:
            pl.when((iz + dz >= 0) & (iz + dz < nz))(action)

    barrier = pltpu.get_barrier_semaphore()

    def greet(dz):
        for k in range(groups):
            if k or dz:
                _, target = place(k, dz)
                pl.semaphore_signal(barrier, inc=1, device_id=target, device_id_type=MESH)

    for dz in (0, -1, 1):
        guarded(dz, functools.partial(greet, dz))
    slabs = 1 + (iz > 0).astype(jnp.int32) + (iz < nz - 1).astype(jnp.int32)
    pl.semaphore_wait(barrier, groups * slabs - 1)

    def lift_copy(dz, k):
        group, target = place(k, dz)
        return pltpu.make_async_remote_copy(
            src_ref=blocks.at[group],
            dst_ref=lifted.at[1 - dz, me],
            send_sem=lift_send.at[1 + dz, k],
            recv_sem=lift_recv.at[1 - dz, me],
            device_id=target,
            device_id_type=MESH,
        )

    def arrival(dz, group):
        return pltpu.make_async_remote_copy(
            src_ref=blocks.at[group],
            dst_ref=lifted.at[1 + dz, group],
            send_sem=lift_send.at[1 + dz, 0],
            recv_sem=lift_recv.at[1 + dz, group],
            device_id=(lax.div(group, ny), lax.rem(group, ny), iz),
            device_id_type=MESH,
        )

    def launch(dz):
        for k in range(groups):
            if k or dz:
                lift_copy(dz, k).start()

    for dz in (0, -1, 1):
        guarded(dz, functools.partial(launch, dz))

    lifted[1, me] = blocks[me]
    rows[...] = jnp.zeros_like(rows)

    def row_of(x, y, z):
        return (x + 1) * step_x + (y + 1) * step_y + z + 1

    def land(dz):
        for k in range(groups):
            if k or dz:
                arrival(dz, lax.rem(me + k, groups)).wait_recv()
        for group in range(groups):
            gx, gy = group // ny, group % ny
            block = lifted[1 + dz, group].astype(jnp.float32)
            for i in range(tx):
                for j in range(ty):
                    start = (i * ty + j) * tz
                    first, size, z = {0: (0, tz, 0), -1: (tz - 1, 1, -1), 1: (0, 1, tz)}[dz]
                    target = row_of(gx * tx + i, gy * ty + j, z)
                    rows[target : target + size, 0 : 2 * width] = block[
                        start + first : start + first + size
                    ]

    for dz in (0, -1, 1):
        guarded(dz, functools.partial(land, dz))

    lanes = rows.shape[1]
    per = lanes // width
    lane = lax.broadcasted_iota(jnp.int32, rows.shape, 1) // width
    full = rows[...]
    for which in range(2):
        for k in range(per):
            shift = (k - which) * width % lanes
            turned = pltpu.roll(full, shift, 1) if shift else full
            copies[which * per + k] = jnp.where(lane == k, turned, 0.0)

    taps = [p * step_x + q * step_y + r for p in range(3) for q in range(3) for r in range(3)]

    def patches(which):
        chunks = []
        for first in range(0, 27, per):
            chunk = None
            for k, tap in enumerate(taps[first : first + per]):
                window = copies[which * per + k, tap : tap + count]
                chunk = window if chunk is None else chunk + window
            chunks.append(chunk.astype(jnp.bfloat16))
        return jnp.concatenate(chunks, axis=1)[:, : 27 * width]

    hidden, change = patches(0), patches(1)
    dot = functools.partial(jnp.dot, preferred_element_type=jnp.float32)
    primal = dot(hidden, weight[...])
    tangent = dot(hidden, probe[...]) + dot(change, weight[...])

    cellcount = out.shape[2]
    row = lax.broadcasted_iota(jnp.int32, (count, cellcount), 0)
    cell = lax.broadcasted_iota(jnp.int32, (count, cellcount), 1)
    source = (
        cell // (whole_y * tz) * step_x + cell // tz % whole_y * step_y + cell % tz
    )
    pick = (row == source).astype(jnp.bfloat16)
    for which, value in enumerate((primal, tangent)):
        dense = dot(value.T.astype(jnp.bfloat16), pick).astype(jnp.bfloat16)
        for group in range(groups):
            parts[group, which] = dense[group * owned : (group + 1) * owned]

    def part_copy(k):
        group, target = place(k, 0)
        return pltpu.make_async_remote_copy(
            src_ref=parts.at[group],
            dst_ref=landed.at[me],
            send_sem=part_send.at[k],
            recv_sem=part_recv.at[me],
            device_id=target,
            device_id_type=MESH,
        )

    def part_arrival(k):
        group, target = place(k, 0)
        return pltpu.make_async_remote_copy(
            src_ref=parts.at[group],
            dst_ref=landed.at[group],
            send_sem=part_send.at[k],
            recv_sem=part_recv.at[group],
            device_id=target,
            device_id_type=MESH,
        )

    for k in range(1, groups):
        part_copy(k).start()
    total = parts[me].astype(jnp.float32)
    for k in range(1, groups):
        part_arrival(k).wait_recv()
        total = total + landed[lax.rem(me + k, groups)].astype(jnp.float32)
    out[0] = (total[0] + bias[...]).astype(out.dtype)
    out[1] = total[1].astype(out.dtype)
    for dz, k in plan:
        guarded(dz, lambda: lift_copy(dz, k).wait_send())
    for k in range(1, groups):
        part_copy(k).wait_send()


def last_layer(blocks, weight, probe, bias, tile_shape):
    tx, ty, tz = tile_shape
    (nx, ny) = lax.axis_size("sx"), lax.axis_size("sy")
    groups, cells_in, pair_width = blocks.shape
    width = pair_width // 2
    outputs = weight.shape[1]
    owned = outputs // groups
    step_x = (ny * ty + 1) * (tz + 2)
    count = -(-nx * tx * step_x // 128) * 128
    height = -(-(count + 2 * step_x + 2 * (tz + 2) + 2) // 16) * 16
    cellcount = nx * tx * ny * ty * tz
    lanes = 128
    per = lanes // width
    bf16, f32 = jnp.bfloat16, jnp.float32
    return pl.pallas_call(
        functools.partial(last_kernel, tile_shape),
        out_shape=jax.ShapeDtypeStruct((2, owned, cellcount), bf16),
        in_specs=[VMEM] * 4,
        out_specs=VMEM,
        scratch_shapes=[
            pltpu.VMEM((3, groups, cells_in, pair_width), bf16),
            pltpu.VMEM((1, count, 128), bf16),
            pltpu.VMEM((height, lanes), f32),
            pltpu.VMEM((2 * per, height, lanes), f32),
            pltpu.VMEM((groups, 2, owned, cellcount), bf16),
            pltpu.VMEM((groups, 2, owned, cellcount), bf16),
            pltpu.SemaphoreType.DMA((3, groups)),
            pltpu.SemaphoreType.DMA((3, groups)),
            pltpu.SemaphoreType.DMA((groups,)),
            pltpu.SemaphoreType.DMA((groups,)),
        ],
        compiler_params=pltpu.CompilerParams(
            collective_id=1, has_side_effects=True, vmem_limit_bytes=48 * 2**20
        ),
    )(blocks, weight, probe, bias)


def flat_weight(weight):
    outputs = weight.shape[0]
    return jnp.transpose(weight, (1, 2, 3, 4, 0)).reshape(-1, outputs)


def body(
    density,
    conv1_weight,
    conv1_bias,
    conv1_probe,
    conv2_weight,
    conv2_bias,
    conv2_probe,
    lift_weight,
    lift_bias,
    lift_probe,
    conv3_weight,
    conv3_bias,
    conv3_probe,
):
    channels_in, span_x, span_y, span_z = density.shape
    width_one = conv1_weight.shape[0]
    width_three = lift_weight.shape[0]
    both_first = jnp.concatenate([conv1_weight, conv1_probe], 0)
    padded = with_halo(density, 2)
    pre_both = cells(padded[None], both_first, 1, "NCDHW")[0]
    hidden, probe = swish_pair(pre_both[:width_one] + per_channel(conv1_bias), pre_both[width_one:])
    inside_x = inside_range(span_x + 2, lax.axis_index("sx") * span_x, span_x * lax.axis_size("sx"))
    inside_y = inside_range(span_y + 2, lax.axis_index("sy") * span_y, span_y * lax.axis_size("sy"))
    inside_z = inside_range(span_z + 2, lax.axis_index("sz") * span_z, span_z * lax.axis_size("sz"))
    inside = inside_x[:, None, None] * inside_y[None, :, None] * inside_z[None, None, :]
    pair = jnp.stack(
        [(hidden * inside).astype(jnp.bfloat16), (probe * inside).astype(jnp.bfloat16)]
    )
    both = cells(pair, conv2_weight, 1, "NCDHW")
    extra = cells(pair[:1], conv2_probe, 1, "NCDHW")[0]
    hidden, probe = swish_pair(both[0] + per_channel(conv2_bias), both[1] + extra)
    pair = jnp.stack([hidden.astype(jnp.bfloat16), probe.astype(jnp.bfloat16)])
    both = cells(pair, lift_weight, 4, "NDHWC")
    extra = cells(pair[:1], lift_probe, 4, "NDHWC")[0]
    hidden, probe = swish_pair(both[0] + lift_bias, both[1] + extra)
    stacked = jnp.stack([hidden.astype(jnp.bfloat16), probe.astype(jnp.bfloat16)])
    tile_shape = stacked.shape[1:4]
    groups = lax.axis_size("sx") * lax.axis_size("sy")
    width = width_three // groups
    blocks = stacked.reshape(2, -1, groups, width)
    blocks = jnp.transpose(blocks, (2, 1, 0, 3)).reshape(groups, -1, 2 * width)
    result = last_layer(
        blocks, flat_weight(conv3_weight), flat_weight(conv3_probe), conv3_bias[:, None], tile_shape
    )
    tx, ty, tz = tile_shape
    result = result.reshape(
        2, -1, tx * lax.axis_size("sx"), ty * lax.axis_size("sy"), tz
    )
    return (result[0], result[1])


def solution(mesh):
    placed = (
        P(None, "sx", "sy", "sz"),
        P(),
        P(),
        P(),
        P(),
        P(),
        P(),
        P(),
        P(),
        P(),
        P(None, None, None, None, ("sx", "sy")),
        P(("sx", "sy")),
        P(None, None, None, None, ("sx", "sy")),
    )
    return jax.shard_map(
        body,
        mesh=mesh,
        in_specs=placed,
        out_specs=(P(("sx", "sy"), None, None, "sz"), P(("sx", "sy"), None, None, "sz")),
        check_vma=False,
    )
```

time: 116 us -> 55.8 us (0.48)
  starting transfers between devices: 26.5 us -> 0 us
  waiting for transfers between devices: 23.7 us -> 0 us
  Pallas kernels: 0 us -> 22.7 us
  between operations: 14.7 us -> 0.98 us
  blocking collectives: 10.9 us -> 0 us
  local copies, waits for them, and re-layouts: 16.3 us -> 7.74 us
  matrix products: 14 us -> 16.4 us
  other arithmetic: 9.22 us -> 7.74 us
    ppermute x12 -> x0, starting transfers between devices: 26.5 us -> none  [the longest x6 18.7 us: with_halo(): lax.ppermute(tail, axis, [(i, (i + 1) % count) for i in range(ends)])]
    ppermute x12 -> x0, waiting for transfers between devices: 22.9 us -> none  [the longest x6 19.6 us: with_halo(): lax.ppermute(head, axis, [((i + 1) % count, i) for i in range(ends)])]
    pallas_call x0 -> x2, Pallas kernels: none -> 22.7 us  [the longest x1 12.4 us: last_layer(): pl.pallas_call(functools.partial(last_kernel, tile_shape), out_shape=jax....]
    all_to_all x2 -> x0, blocking collectives: 10.9 us -> none  [the longest x1 7.22 us: body(): lax.all_to_all(totals.astype(jnp.bfloat16), 'sx', split_axis=1, concat_ax...]
    unnamed x38 -> x24, local copies, waits for them, and re-layouts: 5.36 us -> 0.08 us
    mul x4 -> x0, local copies, waits for them, and re-layouts: 5.14 us -> none  [swish_pair(): return (preact * sigmoid_value, derivative * direction)]
    convert_element_type x1, other arithmetic: 0.63 us -> 4.49 us  [body(): (probe * inside).astype(jnp.bfloat16)]
    conv_general_dilated x10 -> x0, local copies, waits for them, and re-layouts: 3.1 us -> none  [cells(): lax.conv_general_dilated(volume, weight, (stride, stride, stride), 'VALID...]
  transfers between devices with their start and end apart: 14 -> 0, of which waited for: 8 -> 0; matrix products, arithmetic and copies ran while one was open for 28% -> 0% of each run, Pallas kernels for 0% -> 0%
where the time goes in v1:
time: 55.8 us; the launch traced here: 55.6 us
  Pallas kernels  22.7 us (41%)
  matrix products  16.4 us (29%)
  local copies, waits for them, and re-layouts  7.74 us (14%)
  other arithmetic  7.74 us (14%)
  between operations  0.98 us (2%)
    conv_general_dilated x5, matrix products, cells(): lax.conv_general_dilated(volume, weight, (stride, stride, stride), 'VALID...  16.4 us
    pallas_call x1, Pallas kernels, last_layer(): pl.pallas_call(functools.partial(last_kernel, tile_shape), out_shape=jax....  12.4 us
    pallas_call x1, Pallas kernels, with_halo(): pl.pallas_call(functools.partial(tiles_kernel, tile.shape, width), out_sh...  10.3 us
    convert_element_type x1, other arithmetic, body(): (probe * inside).astype(jnp.bfloat16)  4.49 us
    another operation x2, local copies, waits for them, and re-layouts, body(): pre_both = cells(padded[None], both_first, 1, 'NCDHW')[0]  3.19 us
    convert_element_type x1, other arithmetic, body(): (hidden * inside).astype(jnp.bfloat16)  2.63 us
    reshape x1, local copies, waits for them, and re-layouts, with_halo(): tile.reshape(flat)  1.56 us
    slice x3, local copies, waits for them, and re-layouts, body(): return (result[0], result[1])  1.45 us

profile of v1, /device:TPU:0, one launch (start us, length us, event | category | flops | bytes accessed | tf_op | source)
XLA Modules:
  0.0 55.6 jit_solution(9421117517904390284)
XLA Ops:
  0.6 0.0 copy-start
  0.6 0.0 copy-start.11
  0.7 0.0 copy-start.10
  0.7 0.1 broadcast_multiply_fusion.1
  0.8 0.1 broadcast_multiply_fusion
  0.9 1.6 %reshape.89.tile = bf16[32,128]{1,0:T(8,128)(2,1)} reshape(bf16[4,8,8,16]{3,2,1,0:T(8,128)(2,1)} %param.13) | data formatting | bytes 16384 | tf_op jit(solution)/shard_map/reshape | solution.py:157
  2.4 10.3 %shard_map.140 = bf16[48,240]{1,0:T(8,128)(2,1)} custom-call(bf16[32,128]{1,0:T(8,128)(2,1)} %reshape.89.tile), custom_call_target="tpu_custom_call" | custom-call | tf_op jit(solution)/shard_map/pallas_call | solution.py:146
  12.7 1.0 %broadcast_in_dim_reshape.3 = bf16[1,4,12,12,20]{4,3,2,1,0:T(8,128)(2,1)S(1)} reshape(bf16[48,240]{1,0:T(8,128)(2,1)} %shard_map.140) | data formatting | bytes 46080 | tf_op jit(solution)/shard_map/broadcast_in_dim;reshape | solution.py:390
  13.7 2.2 %copy.26 = bf16[1,4,12,12,20]{1,0,4,3,2:T(2,128)(2,1)S(1)} copy(bf16[1,4,12,12,20]{4,3,2,1,0:T(8,128)(2,1)S(1)} %broadcast_in_dim_reshape.3) | data formatting | bytes 46080 | tf_op jit(solution)/shard_map/broadcast_in_dim;reshape | solution.py:390
  15.9 0.0 copy-done.11
  16.0 0.0 copy-done.10
  16.0 0.0 copy-start.3
  16.0 5.5 %fusion.7 = f32[1,64,10,10,18]{1,0,4,3,2:T(1,128)S(1)} fusion(bf16[1,4,12,12,20]{1,0,4,3,2:T(2,128)(2,1)S(1)} %copy.26, bf16[32,3,3,3,4]{0,4,3,2,1:T(4,128)(2,1)S(1)} %copy-done.10, bf16[32,3,3,3,4]{0,4,3,2,1:T(4,128)(2,1)S(1)} %copy-done.11), kind=kOutput, calls=%fused_computation.19 | convolution fusion | flops 24910848 | bytes 497664 | tf_op jit(solution)/shard_map/conv_general_dilated | solution.py:22
  21.5 0.0 copy-done.3
  21.5 2.6 %multiply_convert_fusion = (bf16[1,32,10,10,18]{1,0,4,3,2:T(2,128)(2,1)S(1)}, f32[1,32,10,10,18]{1,0,4,3,2:T(1,128)S(1)}) fusion(f32[10,10,18]{2,1,0:T(8,128)S(1)} %broadcast_multiply_fusion, f32[32]{0:T(128)S(1)} %copy-done.3, f32[1,64,10,10,18]{1,0,4,3,2:T(1,128)S(1)} %fusion.7), kind=kLoop, calls=%fused_computation.4 | loop fusion | flops 403200 | bytes 583328 | tf_op jit(solution)/shard_map/convert_element_type | solution.py:397
  24.1 0.0 copy-start.8
  24.2 4.5 %fusion.1 = bf16[1,32,10,10,18]{1,0,4,3,2:T(2,128)(2,1)S(1)} fusion(f32[1,64,10,10,18]{1,0,4,3,2:T(1,128)S(1)} %fusion.7, f32[1,32,10,10,18]{1,0,4,3,2:T(1,128)S(1)} %get-tuple-element.5, f32[10,10,18]{2,1,0:T(8,128)S(1)} %broadcast_multiply_fusion, f32[32]{0:T(128)S(1)} %copy-done.3), kind=kLoop, calls=%fused_computation.6 | loop fusion | flops 460800 | bytes 813728 | tf_op jit(solution)/shard_map/convert_element_type | solution.py:397
  28.7 0.0 copy-done.8
  28.7 5.3 %fusion.2 = f32[2,32,8,8,16]{1,0,4,3,2:T(2,128)S(1)} fusion(bf16[32,3,3,3,32]{4,0,3,2,1:T(8,128)(2,1)S(1)} %copy-done.8, bf16[1,32,10,10,18]{1,0,4,3,2:T(2,128)(2,1)S(1)} %fusion.1, bf16[1,32,10,10,18]{1,0,4,3,2:T(2,128)(2,1)S(1)} %get-tuple-element.4), kind=kOutput, calls=%fused_computation.7 | convolution fusion | flops 113707008 | bytes 547840 | tf_op jit(solution)/shard_map/conv_general_dilated | solution.py:22
  34.0 0.0 copy-start.9
  34.0 1.0 %fusion.12 = (f32[1,32,8,8,16]{1,0,4,3,2:T(1,128)S(1)}, f32[1,32,8,8,16]{1,0,4,3,2:T(1,128)S(1)}) fusion(f32[2,32,8,8,16]{1,0,4,3,2:T(2,128)S(1)} %fusion.2), kind=kLoop, calls=%fused_computation.33 | loop fusion | bytes 524288 | tf_op jit(solution)/shard_map/slice | solution.py:401
  35.0 0.0 copy-done.9
  35.1 0.0 copy-start.5
  35.1 3.6 %fusion.15 = f32[1,32,8,8,16]{1,0,4,3,2:T(1,128)S(1)} fusion(bf16[1,32,10,10,18]{1,0,4,3,2:T(2,128)(2,1)S(1)} %get-tuple-element.4, bf16[32,3,3,3,32]{4,0,3,2,1:T(8,128)(2,1)S(1)} %copy-done.9), kind=kOutput, calls=%fused_computation.36 | convolution fusion | flops 56623104 | bytes 301568 | tf_op jit(solution)/shard_map/conv_general_dilated | solution.py:22
  38.6 0.0 copy-done.5
  38.7 0.3 multiply_convert_fusion.2
  38.9 0.1 pad_maximum_fusion.2
  39.1 0.0 copy-done
  39.1 0.0 copy-start.7
  39.1 1.1 %fusion.3 = f32[2,2,2,4,256]{4,0,3,2,1:T(2,128)S(1)} fusion(bf16[256,4,4,4,32]{0,4,3,2,1:T(8,128)(2,1)S(1)} %copy-done, bf16[2,32,8,8,16]{1,4,3,2,0:T(8,128)(2,1)S(1)} %pad_maximum_fusion.2), kind=kOutput, calls=%fused_computation.12 | convolution fusion | flops 33554432 | bytes 1212416 | tf_op jit(solution)/shard_map/conv_general_dilated | solution.py:22
  40.2 0.0 copy-start.4
  40.2 0.0 copy-start.6
  40.2 0.0 copy-start.1
  40.3 0.0 copy-start.2
  40.3 0.0 copy-done.7
  40.3 0.8 %fusion.5 = f32[1,2,2,4,256]{4,0,3,2,1:T(1,128)S(1)} fusion(bf16[256,4,4,4,32]{0,4,3,2,1:T(8,128)(2,1)S(1)} %copy-done.7, bf16[1,32,8,8,16]{1,4,3,2,0:T(8,128)(2,1)S(1)} %get-tuple-element.8), kind=kOutput, calls=%fused_computation.14 | convolution fusion | flops 16777216 | bytes 1130496 | tf_op jit(solution)/shard_map/conv_general_dilated | solution.py:22
  41.2 0.0 copy-done.4
  41.2 0.1 stack.21
  41.3 0.1 stack.22
  41.4 0.1 copy.35
  41.5 0.1 reshape.90.blocks
  41.6 0.0 copy-done.6
  41.6 0.1 copy.36.bias
  41.7 0.0 copy-done.1
  41.7 0.0 copy-done.2
  41.7 12.4 %shard_map.141 = bf16[2,32,128]{2,1,0:T(8,128)(2,1)S(1)} custom-call(bf16[8,16,64]{2,1,0:T(8,128)(2,1)S(1)} %reshape.90.blocks, bf16[864,256]{1,0:T(8,128)(2,1)S(1)} %bitcast.22, bf16[864,256]{1,0:T(8,128)(2,1)S(1)} %bitcast.23, f32[32,1]{1,0:T(8,128)S(1)} %copy.36.bias), custom_call_target="tpu_custom_call" | custom-call | tf_op jit(solution)/shard_map/pallas_call | solution.py:342
  54.1 0.7 %copy.37 = bf16[1,32,128]{1,2,0:T(8,128)(2,1)} copy(bf16[1,32,128]{2,1,0:T(8,128)(2,1)S(1)} %get-tuple-element.15) | data formatting | bytes 16384 | tf_op jit(solution)/shard_map/slice | solution.py:419
  54.9 0.7 %copy.38 = bf16[1,32,128]{1,2,0:T(8,128)(2,1)} copy(bf16[1,32,128]{2,1,0:T(8,128)(2,1)S(1)} %get-tuple-element.14) | data formatting | bytes 16384 | tf_op jit(solution)/shard_map/slice | solution.py:419
  (6 shorter events, 0.1 us)
Async XLA Ops:
  0.6 38.4 %copy-start = (bf16[256,4,4,4,32]{0,4,3,2,1:T(8,128)(2,1)S(1)}, bf16[256,4,4,4,32]{0,4,3,2,1:T(8,128)(2,1)}, u32[]{:S(2)}) copy-start(bf16[256,4,4,4,32]{0,4,3,2,1:T(8,128)(2,1)} %param.20) | copy-start | bytes 3145732
  0.6 15.3 %copy-start.11 = (bf16[32,3,3,3,4]{0,4,3,2,1:T(4,128)(2,1)S(1)}, bf16[32,3,3,3,4]{0,4,3,2,1:T(4,128)(2,1)}, u32[]{:S(2)}) copy-start(bf16[32,3,3,3,4]{0,4,3,2,1:T(4,128)(2,1)} %param.14) | copy-start | bytes 20740
  0.7 15.3 %copy-start.10 = (bf16[32,3,3,3,4]{0,4,3,2,1:T(4,128)(2,1)S(1)}, bf16[32,3,3,3,4]{0,4,3,2,1:T(4,128)(2,1)}, u32[]{:S(2)}) copy-start(bf16[32,3,3,3,4]{0,4,3,2,1:T(4,128)(2,1)} %param.16) | copy-start | bytes 20740
  16.0 5.5 %copy-start.3 = (f32[32]{0:T(128)S(1)}, f32[32]{0:T(128)}, u32[]{:S(2)}) copy-start(f32[32]{0:T(128)} %param.15) | copy-start | bytes 388
  24.1 4.5 %copy-start.8 = (bf16[32,3,3,3,32]{4,0,3,2,1:T(8,128)(2,1)S(1)}, bf16[32,3,3,3,32]{4,0,3,2,1:T(8,128)(2,1)}, u32[]{:S(2)}) copy-start(bf16[32,3,3,3,32]{4,0,3,2,1:T(8,128)(2,1)} %param.17) | copy-start | bytes 165892
  34.0 1.0 %copy-start.9 = (bf16[32,3,3,3,32]{4,0,3,2,1:T(8,128)(2,1)S(1)}, bf16[32,3,3,3,32]{4,0,3,2,1:T(8,128)(2,1)}, u32[]{:S(2)}) copy-start(bf16[32,3,3,3,32]{4,0,3,2,1:T(8,128)(2,1)} %param.19) | copy-start | bytes 165892
  35.1 3.6 %copy-start.5 = (f32[32]{0:T(128)S(1)}, f32[32]{0:T(128)}, u32[]{:S(2)}) copy-start(f32[32]{0:T(128)} %param.18) | copy-start | bytes 388
  39.1 1.2 %copy-start.7 = (bf16[256,4,4,4,32]{0,4,3,2,1:T(8,128)(2,1)S(1)}, bf16[256,4,4,4,32]{0,4,3,2,1:T(8,128)(2,1)}, u32[]{:S(2)}) copy-start(bf16[256,4,4,4,32]{0,4,3,2,1:T(8,128)(2,1)} %param.22) | copy-start | bytes 3145732
  40.2 1.0 %copy-start.4 = (f32[256]{0:T(256)S(1)}, f32[256]{0:T(256)}, u32[]{:S(2)}) copy-start(f32[256]{0:T(256)} %param.21) | copy-start | bytes 3076
  40.2 1.4 %copy-start.6 = (f32[32]{0:T(128)S(1)}, f32[32]{0:T(128)}, u32[]{:S(2)}) copy-start(f32[32]{0:T(128)} %param.24) | copy-start | bytes 388
  40.2 1.5 %copy-start.1 = (bf16[256,3,3,3,32]{0,4,3,2,1:T(8,128)(2,1)S(1)}, bf16[256,3,3,3,32]{0,4,3,2,1:T(8,128)(2,1)}, u32[]{:S(2)}) copy-start(bf16[256,3,3,3,32]{0,4,3,2,1:T(8,128)(2,1)} %param.23) | copy-start | bytes 1327108
  40.3 1.5 %copy-start.2 = (bf16[256,3,3,3,32]{0,4,3,2,1:T(8,128)(2,1)S(1)}, bf16[256,3,3,3,32]{0,4,3,2,1:T(8,128)(2,1)}, u32[]{:S(2)}) copy-start(bf16[256,3,3,3,32]{0,4,3,2,1:T(8,128)(2,1)} %param.25) | copy-start | bytes 1327108

commit v2 on v1

--- a/solution.py
+++ b/solution.py
@@ -24,18 +24,9 @@
         weight,
         (stride, stride, stride),
         "VALID",
-        dimension_numbers=("NCDHW", "ODHWI", out_order),
+        dimension_numbers=("NDHWC", "ODHWI", out_order),
         preferred_element_type=jnp.float32,
     )
-
-
-def per_channel(vector):
-    return vector[:, None, None, None]
-
-
-def inside_range(length, offset, whole):
-    position = jnp.arange(length, dtype=jnp.int32) - 1 + offset
-    return ((position >= 0) & (position < whole)).astype(jnp.float32)
 
 
 def positions(axes):
@@ -52,7 +43,10 @@
     return (lax.broadcasted_iota(jnp.int32, (rows, columns), 1 - dim) == want).astype(jnp.bfloat16)
 
 
-def tiles_kernel(shape, width, tile, out, slots, send_sem, recv_sem):
+def tiles_kernel(
+    shape, tile, weight1, bias1, weight2, bias2, out, slots, flat, send_sem, recv_sem
+):
+    width = 2
     channels, span_x, span_y, span_z = shape
     wide_x, wide_y, wide_z = (span + 2 * width for span in (span_x, span_y, span_z))
     axes = ("sx", "sy", "sz")
@@ -109,10 +103,12 @@
     def line(at_column):
         block, cell = at_column // (channels * span_x), at_column % (channels * span_x)
         x = cell % span_x + width + (block - 1) * span_x
-        return cell // span_x * wide_x + x, (x >= 0) & (x < wide_x)
-
-    columns = one_hot(9 * cells_in, wide_y * wide_z, column, 0)
-    lines = one_hot(channels * wide_x, 3 * channels * span_x, line, 1)
+        return x * deep + cell // span_x, (x >= 0) & (x < wide_x)
+
+    pitch = -(-wide_y * wide_z // 128) * 128
+    deep = weight1.shape[1] // 27
+    columns = one_hot(9 * cells_in, pitch, column, 0)
+    lines = one_hot(deep * wide_x, 3 * channels * span_x, line, 1)
     for i, offset in others:
         ok, target = there(offset)
 
@@ -130,7 +126,44 @@
         [jnp.concatenate([slots[9 * i + j] for j in range(9)], axis=1) for i in range(3)], axis=0
     )
     near = dot(near, columns).astype(jnp.bfloat16)
-    out[...] = dot(lines, near).astype(jnp.bfloat16)
+    near = dot(lines, near)
+    field = jnp.concatenate([near[deep * x : deep * (x + 1)] for x in range(wide_x)], axis=1)
+
+    def patches(values):
+        lanes = values.shape[1]
+        taps = []
+        for q in range(3):
+            for r in range(3):
+                shift = -((q - 1) * wide_z + r - 1) % lanes
+                taps.append(pltpu.roll(values, shift, 1) if shift else values)
+        kept = lanes - 2 * pitch
+        return jnp.concatenate(
+            [tap[:, p * pitch : p * pitch + kept] for p in range(3) for tap in taps], axis=0
+        ).astype(jnp.bfloat16)
+
+    width_one = weight1.shape[0] // 2
+    both = dot(weight1[...], patches(field))
+    hidden, probe = swish_pair(both[:width_one] + bias1[...], both[width_one:])
+    place = lax.broadcasted_iota(jnp.int32, (1, hidden.shape[1]), 1)
+    cell = place % pitch
+    inside = None
+    for here, count, span, index in zip(
+        at, counts, (span_x, span_y, span_z), (place // pitch + 1, cell // wide_z, cell % wide_z)
+    ):
+        index = index - width + here * span
+        one = (index >= 0) & (index < count * span)
+        inside = one if inside is None else inside & one
+    hidden = patches(jnp.where(inside, hidden, 0.0))
+    probe = patches(jnp.where(inside, probe, 0.0))
+    both = dot(weight2[...], hidden)
+    change = both[width_one:] + dot(weight2[:width_one], probe)
+    hidden, probe = swish_pair(both[:width_one] + bias2[...], change)
+    flat[...] = jnp.concatenate([hidden, probe], axis=0).T
+    for x in range(span_x):
+        for y in range(span_y):
+            start = x * pitch + (y + width) * wide_z + width
+            to = (x * span_y + y) * span_z
+            out[to : to + span_z] = flat[start : start + span_z].astype(jnp.bfloat16)
     for i, offset in others:
         ok, target = there(offset)
 
@@ -139,22 +172,26 @@
             copy(i, offset, target).wait_send()
 
 
-def with_halo(tile, width):
+def first_layers(tile, weight1, bias1, weight2, bias2):
     channels, span_x, span_y, span_z = tile.shape
-    wide_x, wide_y, wide_z = (span + 2 * width for span in (span_x, span_y, span_z))
-    flat = (channels * span_x, span_y * span_z)
+    merged = (channels * span_x, span_y * span_z)
+    pitch = -(-(span_y + 4) * (span_z + 4) // 128) * 128
+    pair_width = weight1.shape[0]
     return pl.pallas_call(
-        functools.partial(tiles_kernel, tile.shape, width),
-        out_shape=jax.ShapeDtypeStruct((channels * wide_x, wide_y * wide_z), tile.dtype),
-        in_specs=[VMEM],
+        functools.partial(tiles_kernel, tile.shape),
+        out_shape=jax.ShapeDtypeStruct((span_x * span_y * span_z, pair_width), tile.dtype),
+        in_specs=[VMEM] * 5,
         out_specs=VMEM,
         scratch_shapes=[
-            pltpu.VMEM((len(OFFSETS),) + flat, tile.dtype),
+            pltpu.VMEM((len(OFFSETS),) + merged, tile.dtype),
+            pltpu.VMEM((span_x * pitch, pair_width), jnp.float32),
             pltpu.SemaphoreType.DMA((len(OFFSETS),)),
             pltpu.SemaphoreType.DMA((len(OFFSETS),)),
         ],
-        compiler_params=pltpu.CompilerParams(collective_id=0, has_side_effects=True),
-    )(tile.reshape(flat)).reshape(channels, wide_x, wide_y, wide_z)
+        compiler_params=pltpu.CompilerParams(
+            collective_id=0, has_side_effects=True, vmem_limit_bytes=48 * 2**20
+        ),
+    )(tile.reshape(merged), weight1, bias1, weight2, bias2)
 
 
 def last_kernel(
@@ -386,20 +423,13 @@
     width_one = conv1_weight.shape[0]
     width_three = lift_weight.shape[0]
     both_first = jnp.concatenate([conv1_weight, conv1_probe], 0)
-    padded = with_halo(density, 2)
-    pre_both = cells(padded[None], both_first, 1, "NCDHW")[0]
-    hidden, probe = swish_pair(pre_both[:width_one] + per_channel(conv1_bias), pre_both[width_one:])
-    inside_x = inside_range(span_x + 2, lax.axis_index("sx") * span_x, span_x * lax.axis_size("sx"))
-    inside_y = inside_range(span_y + 2, lax.axis_index("sy") * span_y, span_y * lax.axis_size("sy"))
-    inside_z = inside_range(span_z + 2, lax.axis_index("sz") * span_z, span_z * lax.axis_size("sz"))
-    inside = inside_x[:, None, None] * inside_y[None, :, None] * inside_z[None, None, :]
-    pair = jnp.stack(
-        [(hidden * inside).astype(jnp.bfloat16), (probe * inside).astype(jnp.bfloat16)]
-    )
-    both = cells(pair, conv2_weight, 1, "NCDHW")
-    extra = cells(pair[:1], conv2_probe, 1, "NCDHW")[0]
-    hidden, probe = swish_pair(both[0] + per_channel(conv2_bias), both[1] + extra)
-    pair = jnp.stack([hidden.astype(jnp.bfloat16), probe.astype(jnp.bfloat16)])
+    spare = -channels_in % 8
+    both_first = jnp.pad(both_first, ((0, 0),) * 4 + ((0, spare),)).reshape(2 * width_one, -1)
+    both_second = jnp.concatenate([conv2_weight, conv2_probe], 0).reshape(2 * width_one, -1)
+    fine = first_layers(
+        density, both_first, conv1_bias[:, None], both_second, conv2_bias[:, None]
+    ).reshape(span_x, span_y, span_z, 2, width_one)
+    pair = jnp.transpose(fine, (3, 0, 1, 2, 4))
     both = cells(pair, lift_weight, 4, "NDHWC")
     extra = cells(pair[:1], lift_probe, 4, "NDHWC")[0]
     hidden, probe = swish_pair(both[0] + lift_bias, both[1] + extra)

time: 55.8 us -> 33.5 us (0.60)
  matrix products: 16.4 us -> 1.4 us
  other arithmetic: 7.74 us -> 1.39 us
  local copies, waits for them, and re-layouts: 7.74 us -> 5.9 us
  Pallas kernels: 22.7 us -> 23.6 us
    conv_general_dilated x5 -> x2, matrix products: 16.4 us -> 1.4 us  [cells(): lax.conv_general_dilated(volume, weight, (stride, stride, stride), 'VALID...]
    convert_element_type x5 -> x0, other arithmetic: 7.41 us -> none  [the longest x1 4.49 us: body(): (probe * inside).astype(jnp.bfloat16)]
    another operation x2 -> x0, local copies, waits for them, and re-layouts: 3.19 us -> none  [body(): pre_both = cells(padded[None], both_first, 1, 'NCDHW')[0]]
    unnamed x24 -> x22, local copies, waits for them, and re-layouts: 0.08 us -> 3.03 us
    concatenate x0 -> x2, other arithmetic: none -> 1.34 us  [the longest x1 1.24 us: body(): jnp.concatenate([conv2_weight, conv2_probe], 0).reshape(2 * width_one, -1)]
    slice x1 -> x0, local copies, waits for them, and re-layouts: 1.01 us -> none  [body(): both[0] + per_channel(conv2_bias)]
    reshape x1 -> x4, local copies, waits for them, and re-layouts: 1.56 us -> 0.57 us  [the longest x1 0.24 us: body(): fine = first_layers(density, both_first, conv1_bias[:, None], both_second...]
    pallas_call x1, Pallas kernels: 10.3 us -> 11.2 us  [first_layers(): pl.pallas_call(functools.partial(tiles_kernel, tile.shape), out_shape=jax...]
where the time goes in v2:
time: 33.5 us; the launch traced here: 33.1 us
  Pallas kernels  23.6 us (70%)
  local copies, waits for them, and re-layouts  5.9 us (18%)
  matrix products  1.4 us (4%)
  other arithmetic  1.39 us (4%)
  between operations  0.82 us (2%)
    pallas_call x1, Pallas kernels, last_layer(): pl.pallas_call(functools.partial(last_kernel, tile_shape), out_shape=jax....  12.4 us
    pallas_call x1, Pallas kernels, first_layers(): pl.pallas_call(functools.partial(tiles_kernel, tile.shape), out_shape=jax...  11.2 us
    unnamed x22, local copies, waits for them, and re-layouts  3.03 us
    slice x3, local copies, waits for them, and re-layouts, body(): return (result[0], result[1])  1.45 us
    conv_general_dilated x2, matrix products, cells(): lax.conv_general_dilated(volume, weight, (stride, stride, stride), 'VALID...  1.4 us
    concatenate x1, other arithmetic, body(): jnp.concatenate([conv2_weight, conv2_probe], 0).reshape(2 * width_one, -1)  1.24 us

profile of v2, /device:TPU:0, one launch (start us, length us, event | category | flops | bytes accessed | tf_op | source)
XLA Modules:
  0.0 33.1 jit_solution(6820252604258694126)
XLA Ops:
  0.6 0.0 copy-start
  0.6 1.2 %pad_maximum_fusion = bf16[64,3,3,3,32]{4,0,3,2,1:T(8,128)(2,1)S(1)} fusion(bf16[32,3,3,3,32]{4,0,3,2,1:T(8,128)(2,1)} %param.19, bf16[32,3,3,3,32]{4,0,3,2,1:T(8,128)(2,1)} %param.17), kind=kLoop, calls=%fused_computation.2 | loop fusion | flops 221184 | bytes 221184 | tf_op jit(solution)/shard_map/concatenate | solution.py:428
  1.9 0.2 copy.33
  2.1 0.0 copy-start.4
  2.1 0.0 copy-start.5
  2.1 0.1 copy.36.weight2
  2.3 0.6 %copy-done.4 = bf16[32,3,3,3,4]{0,4,3,2,1:T(4,128)(2,1)S(1)} copy-done((bf16[32,3,3,3,4]{0,4,3,2,1:T(4,128)(2,1)S(1)}, bf16[32,3,3,3,4]{0,4,3,2,1:T(4,128)(2,1)}, u32[]{:S(2)}) %copy-start.4) | copy-done | bytes 6936
  2.9 0.0 copy-done.5
  2.9 0.1 fusion.4
  3.0 0.0 copy-start.3
  3.0 0.1 copy.34.weight1
  3.1 0.0 copy-start.7
  3.1 0.6 %copy-done.7 = f32[32]{0:T(128)S(1)} copy-done((f32[32]{0:T(128)S(1)}, f32[32]{0:T(128)}, u32[]{:S(2)}) %copy-start.7) | copy-done | bytes 152
  3.7 0.1 copy.35.bias1
  3.8 0.0 copy-start.8
  3.8 0.7 %copy-done.8 = f32[32]{0:T(128)S(1)} copy-done((f32[32]{0:T(128)S(1)}, f32[32]{0:T(128)}, u32[]{:S(2)}) %copy-start.8) | copy-done | bytes 152
  4.5 0.1 copy.37.bias2
  4.6 0.0 copy-done.3
  4.6 0.1 reshape.34.tile
  4.7 11.2 %shard_map.140 = bf16[1024,64]{1,0:T(8,128)(2,1)S(1)} custom-call(bf16[32,128]{1,0:T(8,128)(2,1)S(1)} %reshape.34.tile, bf16[64,216]{1,0:T(8,128)(2,1)S(1)} %copy.34.weight1, f32[32,1]{1,0:T(8,128)S(1)} %copy.35.bias1, bf16[64,864]{1,0:T(8,128)(2,1)S(1)} %copy.36.weight2, f32[32,1]{1,0:T(8,128)S(1)} %copy.37.bias2), custom_call_target="tpu_custom_call" | custom-call | tf_op jit(solution)/shard_map/pallas_call | solution.py:180
  15.9 0.2 reshape.37
  16.2 0.0 copy-done
  16.2 0.0 copy-start.10
  16.2 0.7 %fusion.9 = f32[2,2,2,4,256]{4,0,3,2,1:T(2,128)S(1)} fusion(bf16[8,8,16,2,32]{4,3,2,1,0:T(2,128)(2,1)S(1)} %reshape.37, bf16[256,4,4,4,32]{0,4,3,2,1:T(8,128)(2,1)S(1)} %copy-done), kind=kOutput, calls=%fused_computation.16 | convolution fusion | flops 33554432 | bytes 1212416 | tf_op jit(solution)/shard_map/conv_general_dilated | solution.py:22
  17.0 0.4 %copy-done.10 = bf16[256,4,4,4,32]{0,4,3,2,1:T(8,128)(2,1)S(1)} copy-done((bf16[256,4,4,4,32]{0,4,3,2,1:T(8,128)(2,1)S(1)}, bf16[256,4,4,4,32]{0,4,3,2,1:T(8,128)(2,1)}, u32[]{:S(2)}) %copy-start.10) | copy-done | bytes 1048600
  17.4 0.0 copy-start.6
  17.4 0.0 copy-start.2
  17.4 0.7 %fusion = f32[1,2,2,4,256]{4,0,3,2,1:T(1,128)S(1)} fusion(bf16[256,4,4,4,32]{0,4,3,2,1:T(8,128)(2,1)S(1)} %copy-done.10, bf16[2,8,8,16,32]{4,0,3,2,1:T(2,128)(2,1)S(1)} %bitcast.24), kind=kOutput, calls=%fused_computation | convolution fusion | flops 16777216 | bytes 1196032 | tf_op jit(solution)/shard_map/conv_general_dilated | solution.py:22
  18.1 0.0 copy-done.6
  18.1 0.0 copy-start.1
  18.2 0.1 stack.10
  18.3 0.1 stack.9
  18.4 0.1 copy.41
  18.4 0.1 reshape.38.blocks
  18.5 0.0 copy-start.9
  18.6 0.6 %copy-done.9 = f32[32]{0:T(128)S(1)} copy-done((f32[32]{0:T(128)S(1)}, f32[32]{0:T(128)}, u32[]{:S(2)}) %copy-start.9) | copy-done | bytes 152
  19.2 0.1 copy.42.bias
  19.3 0.0 copy-done.2
  19.3 0.0 copy-done.1
  19.3 12.4 %shard_map.141 = bf16[2,32,128]{2,1,0:T(8,128)(2,1)S(1)} custom-call(bf16[8,16,64]{2,1,0:T(8,128)(2,1)S(1)} %reshape.38.blocks, bf16[864,256]{1,0:T(8,128)(2,1)S(1)} %bitcast.21, bf16[864,256]{1,0:T(8,128)(2,1)S(1)} %bitcast.22, f32[32,1]{1,0:T(8,128)S(1)} %copy.42.bias), custom_call_target="tpu_custom_call" | custom-call | tf_op jit(solution)/shard_map/pallas_call | solution.py:379
  31.7 0.7 %copy.43 = bf16[1,32,128]{1,2,0:T(8,128)(2,1)} copy(bf16[1,32,128]{2,1,0:T(8,128)(2,1)S(1)} %get-tuple-element.9) | data formatting | bytes 16384 | tf_op jit(solution)/shard_map/slice | solution.py:449
  32.4 0.7 %copy.44 = bf16[1,32,128]{1,2,0:T(8,128)(2,1)} copy(bf16[1,32,128]{2,1,0:T(8,128)(2,1)S(1)} %get-tuple-element.8) | data formatting | bytes 16384 | tf_op jit(solution)/shard_map/slice | solution.py:449
  (4 shorter events, 0.1 us)
Async XLA Ops:
  0.6 15.6 %copy-start = (bf16[256,4,4,4,32]{0,4,3,2,1:T(8,128)(2,1)S(1)}, bf16[256,4,4,4,32]{0,4,3,2,1:T(8,128)(2,1)}, u32[]{:S(2)}) copy-start(bf16[256,4,4,4,32]{0,4,3,2,1:T(8,128)(2,1)} %param.20) | copy-start | bytes 3145732
  2.1 0.7 %copy-start.4 = (bf16[32,3,3,3,4]{0,4,3,2,1:T(4,128)(2,1)S(1)}, bf16[32,3,3,3,4]{0,4,3,2,1:T(4,128)(2,1)}, u32[]{:S(2)}) copy-start(bf16[32,3,3,3,4]{0,4,3,2,1:T(4,128)(2,1)} %param.16) | copy-start | bytes 20740
  2.1 0.8 %copy-start.5 = (bf16[32,3,3,3,4]{0,4,3,2,1:T(4,128)(2,1)S(1)}, bf16[32,3,3,3,4]{0,4,3,2,1:T(4,128)(2,1)}, u32[]{:S(2)}) copy-start(bf16[32,3,3,3,4]{0,4,3,2,1:T(4,128)(2,1)} %param.14) | copy-start | bytes 20740
  3.0 1.6 %copy-start.3 = (bf16[4,8,8,16]{3,2,1,0:T(8,128)(2,1)S(1)}, bf16[4,8,8,16]{3,2,1,0:T(8,128)(2,1)}, u32[]{:S(2)}) copy-start(bf16[4,8,8,16]{3,2,1,0:T(8,128)(2,1)} %param.13) | copy-start | bytes 24580
  3.1 0.7 %copy-start.7 = (f32[32]{0:T(128)S(1)}, f32[32]{0:T(128)}, u32[]{:S(2)}) copy-start(f32[32]{0:T(128)} %param.15) | copy-start | bytes 388
  3.8 0.7 %copy-start.8 = (f32[32]{0:T(128)S(1)}, f32[32]{0:T(128)}, u32[]{:S(2)}) copy-start(f32[32]{0:T(128)} %param.18) | copy-start | bytes 388
  16.2 1.2 %copy-start.10 = (bf16[256,4,4,4,32]{0,4,3,2,1:T(8,128)(2,1)S(1)}, bf16[256,4,4,4,32]{0,4,3,2,1:T(8,128)(2,1)}, u32[]{:S(2)}) copy-start(bf16[256,4,4,4,32]{0,4,3,2,1:T(8,128)(2,1)} %param.22) | copy-start | bytes 3145732
  17.4 0.7 %copy-start.6 = (f32[256]{0:T(256)S(1)}, f32[256]{0:T(256)}, u32[]{:S(2)}) copy-start(f32[256]{0:T(256)} %param.21) | copy-start | bytes 3076
  17.4 1.9 %copy-start.2 = (bf16[256,3,3,3,32]{0,4,3,2,1:T(8,128)(2,1)S(1)}, bf16[256,3,3,3,32]{0,4,3,2,1:T(8,128)(2,1)}, u32[]{:S(2)}) copy-start(bf16[256,3,3,3,32]{0,4,3,2,1:T(8,128)(2,1)} %param.25) | copy-start | bytes 1327108
  18.1 1.2 %copy-start.1 = (bf16[256,3,3,3,32]{0,4,3,2,1:T(8,128)(2,1)S(1)}, bf16[256,3,3,3,32]{0,4,3,2,1:T(8,128)(2,1)}, u32[]{:S(2)}) copy-start(bf16[256,3,3,3,32]{0,4,3,2,1:T(8,128)(2,1)} %param.23) | copy-start | bytes 1327108
  18.5 0.7 %copy-start.9 = (f32[32]{0:T(128)S(1)}, f32[32]{0:T(128)}, u32[]{:S(2)}) copy-start(f32[32]{0:T(128)} %param.24) | copy-start | bytes 388

commit v3 on v2

--- a/solution.py
+++ b/solution.py
@@ -34,6 +34,14 @@
 
 
 OFFSETS = list(itertools.product((-1, 0, 1), repeat=3))
+
+
+def upright(row):
+    size = row.shape[1]
+    same = lax.broadcasted_iota(jnp.int32, (size, size), 0) == lax.broadcasted_iota(
+        jnp.int32, (size, size), 1
+    )
+    return jnp.sum(jnp.where(same, row, 0.0), axis=1, keepdims=True)
 
 
 def one_hot(rows, columns, source, dim):
@@ -143,7 +151,7 @@
 
     width_one = weight1.shape[0] // 2
     both = dot(weight1[...], patches(field))
-    hidden, probe = swish_pair(both[:width_one] + bias1[...], both[width_one:])
+    hidden, probe = swish_pair(both[:width_one] + upright(bias1[...]), both[width_one:])
     place = lax.broadcasted_iota(jnp.int32, (1, hidden.shape[1]), 1)
     cell = place % pitch
     inside = None
@@ -157,7 +165,7 @@
     probe = patches(jnp.where(inside, probe, 0.0))
     both = dot(weight2[...], hidden)
     change = both[width_one:] + dot(weight2[:width_one], probe)
-    hidden, probe = swish_pair(both[:width_one] + bias2[...], change)
+    hidden, probe = swish_pair(both[:width_one] + upright(bias2[...]), change)
     flat[...] = jnp.concatenate([hidden, probe], axis=0).T
     for x in range(span_x):
         for y in range(span_y):
@@ -195,7 +203,7 @@
 
 
 def last_kernel(
-    tile_shape, blocks, weight, probe, bias, out, lifted, sent, rows, copies, parts, landed,
+    tile_shape, blocks, weight, probe, bias, features, tangents, lifted, sent, rows, copies, parts, landed,
     lift_send, lift_recv, part_send, part_recv,
 ):
     tx, ty, tz = tile_shape
@@ -206,7 +214,7 @@
     whole_y, depth = ny * ty, tz + 2
     step_y, step_x = depth, depth * (whole_y + 1)
     count = sent.shape[1]
-    owned = out.shape[1]
+    cellcount, owned = features.shape
 
     def place(k, dz):
         group = lax.rem(me + k, groups)
@@ -314,7 +322,6 @@
     primal = dot(hidden, weight[...])
     tangent = dot(hidden, probe[...]) + dot(change, weight[...])
 
-    cellcount = out.shape[2]
     row = lax.broadcasted_iota(jnp.int32, (count, cellcount), 0)
     cell = lax.broadcasted_iota(jnp.int32, (count, cellcount), 1)
     source = (
@@ -354,8 +361,8 @@
     for k in range(1, groups):
         part_arrival(k).wait_recv()
         total = total + landed[lax.rem(me + k, groups)].astype(jnp.float32)
-    out[0] = (total[0] + bias[...]).astype(out.dtype)
-    out[1] = total[1].astype(out.dtype)
+    features[...] = (total[0].T + bias[...]).astype(features.dtype)
+    tangents[...] = total[1].T.astype(tangents.dtype)
     for dz, k in plan:
         guarded(dz, lambda: lift_copy(dz, k).wait_send())
     for k in range(1, groups):
@@ -378,9 +385,9 @@
     bf16, f32 = jnp.bfloat16, jnp.float32
     return pl.pallas_call(
         functools.partial(last_kernel, tile_shape),
-        out_shape=jax.ShapeDtypeStruct((2, owned, cellcount), bf16),
+        out_shape=[jax.ShapeDtypeStruct((cellcount, owned), bf16)] * 2,
         in_specs=[VMEM] * 4,
-        out_specs=VMEM,
+        out_specs=[VMEM] * 2,
         scratch_shapes=[
             pltpu.VMEM((3, groups, cells_in, pair_width), bf16),
             pltpu.VMEM((1, count, 128), bf16),
@@ -427,7 +434,7 @@
     both_first = jnp.pad(both_first, ((0, 0),) * 4 + ((0, spare),)).reshape(2 * width_one, -1)
     both_second = jnp.concatenate([conv2_weight, conv2_probe], 0).reshape(2 * width_one, -1)
     fine = first_layers(
-        density, both_first, conv1_bias[:, None], both_second, conv2_bias[:, None]
+        density, both_first, conv1_bias[None], both_second, conv2_bias[None]
     ).reshape(span_x, span_y, span_z, 2, width_one)
     pair = jnp.transpose(fine, (3, 0, 1, 2, 4))
     both = cells(pair, lift_weight, 4, "NDHWC")
@@ -440,13 +447,11 @@
     blocks = stacked.reshape(2, -1, groups, width)
     blocks = jnp.transpose(blocks, (2, 1, 0, 3)).reshape(groups, -1, 2 * width)
     result = last_layer(
-        blocks, flat_weight(conv3_weight), flat_weight(conv3_probe), conv3_bias[:, None], tile_shape
+        blocks, flat_weight(conv3_weight), flat_weight(conv3_probe), conv3_bias[None], tile_shape
     )
     tx, ty, tz = tile_shape
-    result = result.reshape(
-        2, -1, tx * lax.axis_size("sx"), ty * lax.axis_size("sy"), tz
-    )
-    return (result[0], result[1])
+    shape = (tx * lax.axis_size("sx"), ty * lax.axis_size("sy"), tz, -1)
+    return tuple(jnp.transpose(value.reshape(shape), (3, 0, 1, 2)) for value in result)
 
 
 def solution(mesh):

time: 33.5 us -> 32.3 us (0.964)
  local copies, waits for them, and re-layouts: 5.9 us -> 4.46 us
  other arithmetic: 1.39 us -> 2.05 us
    slice x3 -> x0, local copies, waits for them, and re-layouts: 1.45 us -> none  [body(): return (result[0], result[1])]
    reshape x1, local copies, waits for them, and re-layouts: 0.11 us -> 1.05 us  [first_layers(): tile.reshape(merged)]
    concatenate x1, other arithmetic: 0.09 us -> 0.86 us  [body(): both_first = jnp.concatenate([conv1_weight, conv1_probe], 0)]
    unnamed x22 -> x20, local copies, waits for them, and re-layouts: 3.03 us -> 2.35 us
where the time goes in v3:
time: 32.3 us; the launch traced here: 32 us
  Pallas kernels  23.3 us (72%)
  local copies, waits for them, and re-layouts  4.46 us (14%)
  other arithmetic  2.05 us (6%)
  matrix products  1.37 us (4%)
  between operations  0.85 us (3%)
    pallas_call x1, Pallas kernels, last_layer(): pl.pallas_call(functools.partial(last_kernel, tile_shape), out_shape=[jax...  12.2 us
    pallas_call x1, Pallas kernels, first_layers(): pl.pallas_call(functools.partial(tiles_kernel, tile.shape), out_shape=jax...  11.1 us
    unnamed x20, local copies, waits for them, and re-layouts  2.35 us
    conv_general_dilated x2, matrix products, cells(): lax.conv_general_dilated(volume, weight, (stride, stride, stride), 'VALID...  1.37 us
    concatenate x1, other arithmetic, body(): jnp.concatenate([conv2_weight, conv2_probe], 0).reshape(2 * width_one, -1)  1.14 us
    reshape x1, local copies, waits for them, and re-layouts, first_layers(): tile.reshape(merged)  1.05 us
    concatenate x1, other arithmetic, body(): both_first = jnp.concatenate([conv1_weight, conv1_probe], 0)  0.86 us

profile of v3, /device:TPU:0, one launch (start us, length us, event | category | flops | bytes accessed | tf_op | source)
XLA Modules:
  0.0 32.0 jit_solution(5032141965084777520)
XLA Ops:
  0.6 0.0 copy-start
  0.6 0.0 copy-start.6
  0.7 1.1 %reshape.35.tile = bf16[32,128]{1,0:T(8,128)(2,1)S(1)} reshape(bf16[4,8,8,16]{3,2,1,0:T(8,128)(2,1)} %param.13) | data formatting | bytes 16384 | tf_op jit(solution)/shard_map/reshape | solution.py:202
  1.7 0.9 %fusion.4 = bf16[64,3,3,3,8]{0,4,3,2,1:T(8,128)(2,1)S(1)} fusion(bf16[32,3,3,3,4]{0,4,3,2,1:T(4,128)(2,1)} %param.16, bf16[32,3,3,3,4]{0,4,3,2,1:T(4,128)(2,1)} %param.14), kind=kLoop, calls=%fused_computation.7 | loop fusion | flops 96768 | bytes 41472 | tf_op jit(solution)/shard_map/concatenate | solution.py:432
  2.6 0.1 copy.24.weight1
  2.7 0.0 copy-done.6
  2.7 0.0 copy-start.8
  2.7 1.1 %pad_maximum_fusion = bf16[64,3,3,3,32]{4,0,3,2,1:T(8,128)(2,1)S(1)} fusion(bf16[32,3,3,3,32]{4,0,3,2,1:T(8,128)(2,1)S(1)} %copy-done.6, bf16[32,3,3,3,32]{4,0,3,2,1:T(8,128)(2,1)} %param.17), kind=kLoop, calls=%fused_computation.2 | loop fusion | flops 221184 | bytes 221184 | tf_op jit(solution)/shard_map/concatenate | solution.py:435
  3.8 0.2 copy.23
  4.1 0.0 copy-start.3
  4.1 0.0 copy-start.4
  4.1 0.1 copy.25.weight2
  4.2 0.5 %copy-done.3 = f32[32]{0:T(128)S(1)} copy-done((f32[32]{0:T(128)S(1)}, f32[32]{0:T(128)}, u32[]{:S(2)}) %copy-start.3) | copy-done | bytes 152
  4.7 0.0 copy-done.4
  4.7 11.1 %shard_map.140 = bf16[1024,64]{1,0:T(8,128)(2,1)S(1)} custom-call(bf16[32,128]{1,0:T(8,128)(2,1)S(1)} %reshape.35.tile, bf16[64,216]{1,0:T(8,128)(2,1)S(1)} %copy.24.weight1, f32[1,32]{1,0:T(1,128)S(1)} %bitcast.29, bf16[64,864]{1,0:T(8,128)(2,1)S(1)} %copy.25.weight2, f32[1,32]{1,0:T(1,128)S(1)} %bitcast.30), custom_call_target="tpu_custom_call" | custom-call | tf_op jit(solution)/shard_map/pallas_call | solution.py:188
  15.9 0.2 reshape.38
  16.1 0.0 copy-done.8
  16.1 0.6 %fusion = f32[1,2,2,4,256]{4,0,3,2,1:T(1,128)S(1)} fusion(bf16[256,4,4,4,32]{0,4,3,2,1:T(8,128)(2,1)S(1)} %copy-done.8, bf16[2,8,8,16,32]{4,0,3,2,1:T(2,128)(2,1)S(1)} %bitcast.33), kind=kOutput, calls=%fused_computation | convolution fusion | flops 16777216 | bytes 1196032 | tf_op jit(solution)/shard_map/conv_general_dilated | solution.py:22
  16.8 0.0 copy-done
  16.8 0.0 copy-start.7
  16.8 0.0 copy-start.2
  16.8 0.7 %fusion.8 = f32[2,2,2,4,256]{4,0,3,2,1:T(2,128)S(1)} fusion(bf16[8,8,16,2,32]{4,3,2,1,0:T(2,128)(2,1)S(1)} %reshape.38, bf16[256,4,4,4,32]{0,4,3,2,1:T(8,128)(2,1)S(1)} %copy-done), kind=kOutput, calls=%fused_computation.15 | convolution fusion | flops 33554432 | bytes 1212416 | tf_op jit(solution)/shard_map/conv_general_dilated | solution.py:22
  17.6 0.0 copy-start.1
  17.6 0.0 copy-done.7
  17.7 0.1 stack.9
  17.7 0.1 stack.10
  17.9 0.1 copy.29
  17.9 0.0 copy-start.5
  18.0 0.1 reshape.39.blocks
  18.1 0.0 copy-done.2
  18.1 0.5 %copy-done.1 = bf16[256,3,3,3,32]{0,4,3,2,1:T(8,128)(2,1)S(1)} copy-done((bf16[256,3,3,3,32]{0,4,3,2,1:T(8,128)(2,1)S(1)}, bf16[256,3,3,3,32]{0,4,3,2,1:T(8,128)(2,1)}, u32[]{:S(2)}) %copy-start.1) | copy-done | bytes 442392
  18.6 0.0 copy-done.5
  18.6 12.2 %shard_map.141 = (bf16[128,32]{1,0:T(8,128)(2,1)S(1)}, bf16[128,32]{1,0:T(8,128)(2,1)S(1)}) custom-call(bf16[8,16,64]{2,1,0:T(8,128)(2,1)S(1)} %reshape.39.blocks, bf16[864,256]{1,0:T(8,128)(2,1)S(1)} %bitcast.25, bf16[864,256]{1,0:T(8,128)(2,1)S(1)} %bitcast.26, f32[1,32]{1,0:T(1,128)S(1)} %bitcast.31), custom_call_target="tpu_custom_call" | custom-call | tf_op jit(solution)/shard_map/pallas_call | solution.py:386
  30.8 0.6 %copy.51 = bf16[32,8,4,4]{0,3,2,1:T(4,128)(2,1)} copy(bf16[32,8,4,4]{0,3,2,1:T(4,128)(2,1)S(1)} %bitcast.28) | data formatting | bytes 16384
  31.4 0.6 %copy.52 = bf16[32,8,4,4]{0,3,2,1:T(4,128)(2,1)} copy(bf16[32,8,4,4]{0,3,2,1:T(4,128)(2,1)S(1)} %bitcast.27) | data formatting | bytes 16384
  (3 shorter events, 0.1 us)
Async XLA Ops:
  0.6 16.2 %copy-start = (bf16[256,4,4,4,32]{0,4,3,2,1:T(8,128)(2,1)S(1)}, bf16[256,4,4,4,32]{0,4,3,2,1:T(8,128)(2,1)}, u32[]{:S(2)}) copy-start(bf16[256,4,4,4,32]{0,4,3,2,1:T(8,128)(2,1)} %param.20) | copy-start | bytes 3145732
  0.6 2.0 %copy-start.6 = (bf16[32,3,3,3,32]{4,0,3,2,1:T(8,128)(2,1)S(1)}, bf16[32,3,3,3,32]{4,0,3,2,1:T(8,128)(2,1)}, u32[]{:S(2)}) copy-start(bf16[32,3,3,3,32]{4,0,3,2,1:T(8,128)(2,1)} %param.19) | copy-start | bytes 165892
  2.7 13.4 %copy-start.8 = (bf16[256,4,4,4,32]{0,4,3,2,1:T(8,128)(2,1)S(1)}, bf16[256,4,4,4,32]{0,4,3,2,1:T(8,128)(2,1)}, u32[]{:S(2)}) copy-start(bf16[256,4,4,4,32]{0,4,3,2,1:T(8,128)(2,1)} %param.22) | copy-start | bytes 3145732
  4.1 0.7 %copy-start.3 = (f32[32]{0:T(128)S(1)}, f32[32]{0:T(128)}, u32[]{:S(2)}) copy-start(f32[32]{0:T(128)} %param.15) | copy-start | bytes 388
  4.1 0.7 %copy-start.4 = (f32[32]{0:T(128)S(1)}, f32[32]{0:T(128)}, u32[]{:S(2)}) copy-start(f32[32]{0:T(128)} %param.18) | copy-start | bytes 388
  16.8 0.8 %copy-start.7 = (f32[256]{0:T(256)S(1)}, f32[256]{0:T(256)}, u32[]{:S(2)}) copy-start(f32[256]{0:T(256)} %param.21) | copy-start | bytes 3076
  16.8 1.3 %copy-start.2 = (bf16[256,3,3,3,32]{0,4,3,2,1:T(8,128)(2,1)S(1)}, bf16[256,3,3,3,32]{0,4,3,2,1:T(8,128)(2,1)}, u32[]{:S(2)}) copy-start(bf16[256,3,3,3,32]{0,4,3,2,1:T(8,128)(2,1)} %param.25) | copy-start | bytes 1327108
  17.6 1.0 %copy-start.1 = (bf16[256,3,3,3,32]{0,4,3,2,1:T(8,128)(2,1)S(1)}, bf16[256,3,3,3,32]{0,4,3,2,1:T(8,128)(2,1)}, u32[]{:S(2)}) copy-start(bf16[256,3,3,3,32]{0,4,3,2,1:T(8,128)(2,1)} %param.23) | copy-start | bytes 1327108
  17.9 0.7 %copy-start.5 = (f32[32]{0:T(128)S(1)}, f32[32]{0:T(128)}, u32[]{:S(2)}) copy-start(f32[32]{0:T(128)} %param.24) | copy-start | bytes 388

commit v4 on v3

--- a/solution.py
+++ b/solution.py
@@ -52,7 +52,7 @@
 
 
 def tiles_kernel(
-    shape, tile, weight1, bias1, weight2, bias2, out, slots, flat, send_sem, recv_sem
+    shape, tile, weight1, bias1, weight2, probe2, bias2, out, slots, flat, send_sem, recv_sem
 ):
     width = 2
     channels, span_x, span_y, span_z = shape
@@ -163,9 +163,8 @@
         inside = one if inside is None else inside & one
     hidden = patches(jnp.where(inside, hidden, 0.0))
     probe = patches(jnp.where(inside, probe, 0.0))
-    both = dot(weight2[...], hidden)
-    change = both[width_one:] + dot(weight2[:width_one], probe)
-    hidden, probe = swish_pair(both[:width_one] + upright(bias2[...]), change)
+    change = dot(probe2[...], hidden) + dot(weight2[...], probe)
+    hidden, probe = swish_pair(dot(weight2[...], hidden) + upright(bias2[...]), change)
     flat[...] = jnp.concatenate([hidden, probe], axis=0).T
     for x in range(span_x):
         for y in range(span_y):
@@ -180,7 +179,7 @@
             copy(i, offset, target).wait_send()
 
 
-def first_layers(tile, weight1, bias1, weight2, bias2):
+def first_layers(tile, weight1, bias1, weight2, probe2, bias2):
     channels, span_x, span_y, span_z = tile.shape
     merged = (channels * span_x, span_y * span_z)
     pitch = -(-(span_y + 4) * (span_z + 4) // 128) * 128
@@ -188,7 +187,7 @@
     return pl.pallas_call(
         functools.partial(tiles_kernel, tile.shape),
         out_shape=jax.ShapeDtypeStruct((span_x * span_y * span_z, pair_width), tile.dtype),
-        in_specs=[VMEM] * 5,
+        in_specs=[VMEM] * 6,
         out_specs=VMEM,
         scratch_shapes=[
             pltpu.VMEM((len(OFFSETS),) + merged, tile.dtype),
@@ -199,7 +198,7 @@
         compiler_params=pltpu.CompilerParams(
             collective_id=0, has_side_effects=True, vmem_limit_bytes=48 * 2**20
         ),
-    )(tile.reshape(merged), weight1, bias1, weight2, bias2)
+    )(tile.reshape(merged), weight1, bias1, weight2, probe2, bias2)
 
 
 def last_kernel(
@@ -432,9 +431,13 @@
     both_first = jnp.concatenate([conv1_weight, conv1_probe], 0)
     spare = -channels_in % 8
     both_first = jnp.pad(both_first, ((0, 0),) * 4 + ((0, spare),)).reshape(2 * width_one, -1)
-    both_second = jnp.concatenate([conv2_weight, conv2_probe], 0).reshape(2 * width_one, -1)
     fine = first_layers(
-        density, both_first, conv1_bias[None], both_second, conv2_bias[None]
+        density,
+        both_first,
+        conv1_bias[None],
+        conv2_weight.reshape(width_one, -1),
+        conv2_probe.reshape(width_one, -1),
+        conv2_bias[None],
     ).reshape(span_x, span_y, span_z, 2, width_one)
     pair = jnp.transpose(fine, (3, 0, 1, 2, 4))
     both = cells(pair, lift_weight, 4, "NDHWC")

time: 32.3 us -> 32.6 us (level)
  other arithmetic: 2.05 us -> 0.91 us
  local copies, waits for them, and re-layouts: 4.46 us -> 5.47 us
  Pallas kernels: 23.3 us -> 23.7 us
    concatenate x1 -> x0, other arithmetic: 1.14 us -> none  [body(): jnp.concatenate([conv2_weight, conv2_probe], 0).reshape(2 * width_one, -1)]
    unnamed x20 -> x24, local copies, waits for them, and re-layouts: 2.35 us -> 3.33 us
    pallas_call x1, Pallas kernels: 11.1 us -> 11.6 us  [first_layers(): pl.pallas_call(functools.partial(tiles_kernel, tile.shape), out_shape=jax...]
where the time goes in v4:
time: 32.6 us; the launch traced here: 32.4 us
  Pallas kernels  23.7 us (73%)
  local copies, waits for them, and re-layouts  5.47 us (17%)
  matrix products  1.37 us (4%)
  other arithmetic  0.91 us (3%)
  between operations  0.86 us (3%)
    pallas_call x1, Pallas kernels, last_layer(): pl.pallas_call(functools.partial(last_kernel, tile_shape), out_shape=[jax...  12.2 us
    pallas_call x1, Pallas kernels, first_layers(): pl.pallas_call(functools.partial(tiles_kernel, tile.shape), out_shape=jax...  11.6 us
    unnamed x24, local copies, waits for them, and re-layouts  3.33 us
    conv_general_dilated x2, matrix products, cells(): lax.conv_general_dilated(volume, weight, (stride, stride, stride), 'VALID...  1.37 us
    reshape x1, local copies, waits for them, and re-layouts, first_layers(): tile.reshape(merged)  1.05 us
    concatenate x1, other arithmetic, body(): both_first = jnp.concatenate([conv1_weight, conv1_probe], 0)  0.86 us

profile of v4, /device:TPU:0, one launch (start us, length us, event | category | flops | bytes accessed | tf_op | source)
XLA Modules:
  0.0 32.4 jit_solution(1730930815536508664)
XLA Ops:
  0.6 0.0 copy-start
  0.6 0.0 copy-start.6
  0.7 1.1 %reshape.38.tile = bf16[32,128]{1,0:T(8,128)(2,1)S(1)} reshape(bf16[4,8,8,16]{3,2,1,0:T(8,128)(2,1)} %param.13) | data formatting | bytes 16384 | tf_op jit(solution)/shard_map/reshape | solution.py:201
  1.7 0.9 %fusion.4 = bf16[64,3,3,3,8]{0,4,3,2,1:T(8,128)(2,1)S(1)} fusion(bf16[32,3,3,3,4]{0,4,3,2,1:T(4,128)(2,1)} %param.16, bf16[32,3,3,3,4]{0,4,3,2,1:T(4,128)(2,1)} %param.14), kind=kLoop, calls=%fused_computation.6 | loop fusion | flops 96768 | bytes 41472 | tf_op jit(solution)/shard_map/concatenate | solution.py:431
  2.6 0.1 copy.26.weight1
  2.7 0.0 copy-done.6
  2.7 0.2 copy.24
  2.8 0.0 copy-start.7
  2.9 0.2 reshape.40.weight2
  3.0 0.7 %copy-done.7 = bf16[32,3,3,3,32]{4,0,3,2,1:T(8,128)(2,1)S(1)} copy-done((bf16[32,3,3,3,32]{4,0,3,2,1:T(8,128)(2,1)S(1)}, bf16[32,3,3,3,32]{4,0,3,2,1:T(8,128)(2,1)}, u32[]{:S(2)}) %copy-start.7) | copy-done | bytes 55320
  3.8 0.2 copy.25
  3.9 0.0 copy-start.3
  3.9 0.0 copy-start.4
  4.0 0.0 copy-start.9
  4.0 0.2 reshape.41.probe2
  4.2 0.4 %copy-done.3 = f32[32]{0:T(128)S(1)} copy-done((f32[32]{0:T(128)S(1)}, f32[32]{0:T(128)}, u32[]{:S(2)}) %copy-start.3) | copy-done | bytes 152
  4.6 0.0 copy-done.4
  4.6 11.6 %shard_map.140 = bf16[1024,64]{1,0:T(8,128)(2,1)S(1)} custom-call(bf16[32,128]{1,0:T(8,128)(2,1)S(1)} %reshape.38.tile, bf16[64,216]{1,0:T(8,128)(2,1)S(1)} %copy.26.weight1, f32[1,32]{1,0:T(1,128)S(1)} %bitcast.28, bf16[32,864]{1,0:T(8,128)(2,1)S(1)} %reshape.40.weight2, bf16[32,864]{1,0:T(8,128)(2,1)S(1)} %reshape.41.probe2, f32[1,32]{1,0:T(1,128)S(1)} %bitcast.29), custom_call_target="tpu_custom_call" | custom-call | tf_op jit(solution)/shard_map/pallas_call | solution.py:187
  16.2 0.2 reshape.42
  16.4 0.0 copy-done.9
  16.5 0.6 %fusion = f32[1,2,2,4,256]{4,0,3,2,1:T(1,128)S(1)} fusion(bf16[256,4,4,4,32]{0,4,3,2,1:T(8,128)(2,1)S(1)} %copy-done.9, bf16[2,8,8,16,32]{4,0,3,2,1:T(2,128)(2,1)S(1)} %bitcast.31), kind=kOutput, calls=%fused_computation | convolution fusion | flops 16777216 | bytes 1196032 | tf_op jit(solution)/shard_map/conv_general_dilated | solution.py:22
  17.1 0.0 copy-done
  17.1 0.0 copy-start.8
  17.1 0.0 copy-start.2
  17.1 0.7 %fusion.8 = f32[2,2,2,4,256]{4,0,3,2,1:T(2,128)S(1)} fusion(bf16[8,8,16,2,32]{4,3,2,1,0:T(2,128)(2,1)S(1)} %reshape.42, bf16[256,4,4,4,32]{0,4,3,2,1:T(8,128)(2,1)S(1)} %copy-done), kind=kOutput, calls=%fused_computation.14 | convolution fusion | flops 33554432 | bytes 1212416 | tf_op jit(solution)/shard_map/conv_general_dilated | solution.py:22
  17.9 0.0 copy-start.1
  17.9 0.0 copy-done.8
  18.0 0.1 stack.9
  18.1 0.1 stack.10
  18.2 0.1 copy.30
  18.3 0.0 copy-start.5
  18.3 0.1 reshape.43.blocks
  18.4 0.0 copy-done.2
  18.4 0.5 %copy-done.1 = bf16[256,3,3,3,32]{0,4,3,2,1:T(8,128)(2,1)S(1)} copy-done((bf16[256,3,3,3,32]{0,4,3,2,1:T(8,128)(2,1)S(1)}, bf16[256,3,3,3,32]{0,4,3,2,1:T(8,128)(2,1)}, u32[]{:S(2)}) %copy-start.1) | copy-done | bytes 442392
  18.9 0.0 copy-done.5
  18.9 12.2 %shard_map.141 = (bf16[128,32]{1,0:T(8,128)(2,1)S(1)}, bf16[128,32]{1,0:T(8,128)(2,1)S(1)}) custom-call(bf16[8,16,64]{2,1,0:T(8,128)(2,1)S(1)} %reshape.43.blocks, bf16[864,256]{1,0:T(8,128)(2,1)S(1)} %bitcast.24, bf16[864,256]{1,0:T(8,128)(2,1)S(1)} %bitcast.25, f32[1,32]{1,0:T(1,128)S(1)} %bitcast.30), custom_call_target="tpu_custom_call" | custom-call | tf_op jit(solution)/shard_map/pallas_call | solution.py:385
  31.1 0.6 %copy.52 = bf16[32,8,4,4]{0,3,2,1:T(4,128)(2,1)} copy(bf16[32,8,4,4]{0,3,2,1:T(4,128)(2,1)S(1)} %bitcast.27) | data formatting | bytes 16384
  31.7 0.6 %copy.53 = bf16[32,8,4,4]{0,3,2,1:T(4,128)(2,1)} copy(bf16[32,8,4,4]{0,3,2,1:T(4,128)(2,1)S(1)} %bitcast.26) | data formatting | bytes 16384
  (3 shorter events, 0.1 us)
Async XLA Ops:
  0.6 16.5 %copy-start = (bf16[256,4,4,4,32]{0,4,3,2,1:T(8,128)(2,1)S(1)}, bf16[256,4,4,4,32]{0,4,3,2,1:T(8,128)(2,1)}, u32[]{:S(2)}) copy-start(bf16[256,4,4,4,32]{0,4,3,2,1:T(8,128)(2,1)} %param.20) | copy-start | bytes 3145732
  0.6 2.0 %copy-start.6 = (bf16[32,3,3,3,32]{4,0,3,2,1:T(8,128)(2,1)S(1)}, bf16[32,3,3,3,32]{4,0,3,2,1:T(8,128)(2,1)}, u32[]{:S(2)}) copy-start(bf16[32,3,3,3,32]{4,0,3,2,1:T(8,128)(2,1)} %param.17) | copy-start | bytes 165892
  2.8 0.9 %copy-start.7 = (bf16[32,3,3,3,32]{4,0,3,2,1:T(8,128)(2,1)S(1)}, bf16[32,3,3,3,32]{4,0,3,2,1:T(8,128)(2,1)}, u32[]{:S(2)}) copy-start(bf16[32,3,3,3,32]{4,0,3,2,1:T(8,128)(2,1)} %param.19) | copy-start | bytes 165892
  3.9 0.7 %copy-start.3 = (f32[32]{0:T(128)S(1)}, f32[32]{0:T(128)}, u32[]{:S(2)}) copy-start(f32[32]{0:T(128)} %param.15) | copy-start | bytes 388
  3.9 0.7 %copy-start.4 = (f32[32]{0:T(128)S(1)}, f32[32]{0:T(128)}, u32[]{:S(2)}) copy-start(f32[32]{0:T(128)} %param.18) | copy-start | bytes 388
  4.0 12.5 %copy-start.9 = (bf16[256,4,4,4,32]{0,4,3,2,1:T(8,128)(2,1)S(1)}, bf16[256,4,4,4,32]{0,4,3,2,1:T(8,128)(2,1)}, u32[]{:S(2)}) copy-start(bf16[256,4,4,4,32]{0,4,3,2,1:T(8,128)(2,1)} %param.22) | copy-start | bytes 3145732
  17.1 0.8 %copy-start.8 = (f32[256]{0:T(256)S(1)}, f32[256]{0:T(256)}, u32[]{:S(2)}) copy-start(f32[256]{0:T(256)} %param.21) | copy-start | bytes 3076
  17.1 1.3 %copy-start.2 = (bf16[256,3,3,3,32]{0,4,3,2,1:T(8,128)(2,1)S(1)}, bf16[256,3,3,3,32]{0,4,3,2,1:T(8,128)(2,1)}, u32[]{:S(2)}) copy-start(bf16[256,3,3,3,32]{0,4,3,2,1:T(8,128)(2,1)} %param.25) | copy-start | bytes 1327108
  17.9 1.0 %copy-start.1 = (bf16[256,3,3,3,32]{0,4,3,2,1:T(8,128)(2,1)S(1)}, bf16[256,3,3,3,32]{0,4,3,2,1:T(8,128)(2,1)}, u32[]{:S(2)}) copy-start(bf16[256,3,3,3,32]{0,4,3,2,1:T(8,128)(2,1)} %param.23) | copy-start | bytes 1327108
  18.3 0.7 %copy-start.5 = (f32[32]{0:T(128)S(1)}, f32[32]{0:T(128)}, u32[]{:S(2)}) copy-start(f32[32]{0:T(128)} %param.24) | copy-start | bytes 388
